TPU v7x, 32 devices: a whole 2x2x4 slice. The times are simulated.
32 devices in a mesh: dp: 4 (over x, core), seq: 2 (over y), tensor: 4 (over z).
Axes of the slice: x: 2, y: 2, z: 4, core: 2. Of those that a mesh axis runs over, the one named last changes fastest.
Arguments:
- lower: bfloat16 [2560, 4096], P(('dp', 'seq', 'tensor')), may hold values from -6 to 6
- upper: bfloat16 [2560, 4096], P(('dp', 'seq', 'tensor')), may hold values from -4 to 4
- grad_upper: bfloat16 [2560, 4096], P(('dp', 'seq', 'tensor')), may hold values from -6 to 6
- grad_lower: bfloat16 [2560, 4096], P(('dp', 'seq', 'tensor')), may hold values from -4 to 4
- positions: int32 [4, 640], P('dp'), may hold values from 0 to 399, as said below
- norm_gain: float32 [4096], replicated, may hold values from 0.1 to 1.9
- w_query: bfloat16 [4096, 4096], P(None, 'tensor'), may hold values from -1.875 to 1.875
- w_key: bfloat16 [4096, 1024], P(None, 'tensor'), may hold values from -0.09375 to 0.09375
- w_value: bfloat16 [4096, 1024], P(None, 'tensor'), may hold values from -0.09375 to 0.09375
- w_out: bfloat16 [4096, 4096], P('tensor'), may hold values from -0.375 to 0.375
Outputs:
- restored: bfloat16 [2560, 4096], P(('dp', 'seq', 'tensor'))
- grad_lower_in: bfloat16 [2560, 4096], P(('dp', 'seq', 'tensor'))
- grad_query: float32 [4096, 4096], P(('dp', 'seq'), 'tensor')
- grad_key: float32 [4096, 1024], P(('dp', 'seq'), 'tensor')
- grad_value: float32 [4096, 1024], P(('dp', 'seq'), 'tensor')
- grad_out: float32 [4096, 4096], P('tensor', ('dp', 'seq'))
Inputs may be any that keep to these rules, and one draw needn't show every extreme that they name: `positions`: each group's row packs three documents in order; a position counts tokens from its document's start; the second document has exactly 400 tokens and starts before 3 * 80.
All inputs are finite; a program needn't handle non-finite values.
Results may differ from a plain program's by a relative error of at most 0.02.
The roundings to bfloat16 on the way count: a program that leaves them out, or rounds other values in their place, can miss the bound.
Values may be sent and summed in bfloat16 or wider, within the bound.
A program may use at most 192 MiB of HBM per device.

v0:
```python
import math

import jax
import jax.numpy as jnp
from jax import lax
from jax.sharding import PartitionSpec as P

HD = 128


def tables(positions_row):
    half = HD // 2
    freq = jnp.exp(jnp.arange(half, dtype=jnp.float32) * (-2.0 * math.log(10000.0) / HD))
    angle = positions_row.astype(jnp.float32)[:, None] * freq[None, :]
    return (jnp.cos(angle), jnp.sin(angle))


def rotate(values, cosine, sine):
    half = values.shape[-1] // 2
    first = values[..., :half]
    second = values[..., half:]
    cosine = cosine[:, None, :]
    sine = sine[:, None, :]
    return jnp.concatenate([first * cosine - second * sine, second * cosine + first * sine], -1)


def unrotate(values, cosine, sine):
    half = values.shape[-1] // 2
    first = values[..., :half]
    second = values[..., half:]
    cosine = cosine[:, None, :]
    sine = sine[:, None, :]
    return jnp.concatenate([first * cosine + second * sine, second * cosine - first * sine], -1)


def norm_rows(rows_in, norm_gain):
    rows_f = rows_in.astype(jnp.float32)
    inverse = lax.rsqrt(jnp.mean(rows_f * rows_f, -1, keepdims=True) + 1e-05)
    normed = rows_f * inverse
    return (normed, inverse, (normed * norm_gain).astype(jnp.bfloat16))


def project_keys(hidden_rows, w_key, w_value, cosine, sine):
    count = hidden_rows.shape[0]
    kv_local = w_key.shape[1] // HD
    keys = jnp.dot(hidden_rows, w_key, preferred_element_type=jnp.float32).reshape(
        count, kv_local, HD
    )
    keys = rotate(keys, cosine, sine).astype(jnp.bfloat16).reshape(count, -1)
    values = jnp.dot(hidden_rows, w_value, preferred_element_type=jnp.float32).astype(jnp.bfloat16)
    return (keys, values)


def contract_last(left, right):
    return lax.dot_general(
        left, right, (((1,), (1,)), ((), ())), preferred_element_type=jnp.float32
    )


def contract_first(left, right):
    return lax.dot_general(
        left, right, (((0,), (0,)), ((), ())), preferred_element_type=jnp.float32
    )


def shards(
    lower, upper, grad_upper, grad_lower, positions, norm_gain, w_query, w_key, w_value, w_out
):
    rows = lower.shape[0]
    n_tensor = lax.axis_size("tensor")
    n_seq = lax.axis_size("seq")
    half_rows = rows * n_tensor
    length = half_rows * n_seq
    kv_local = w_key.shape[1] // HD
    q_width = w_query.shape[1]
    scale = HD ** (-0.5)
    base = lax.axis_index("seq") * half_rows
    sequence_pos = positions[0]
    own_pos = lax.dynamic_slice_in_dim(sequence_pos, base, half_rows, 0)
    cos_own, sin_own = tables(own_pos)
    every_row = lax.all_gather(lower, ("seq", "tensor"), axis=0, tiled=True)
    normed_all, inverse_all, hidden_all = norm_rows(every_row, norm_gain)
    cos_all, sin_all = tables(sequence_pos)
    keys, values = project_keys(hidden_all, w_key, w_value, cos_all, sin_all)
    hidden = lax.dynamic_slice_in_dim(hidden_all, base, half_rows, 0)
    queries = jnp.dot(hidden, w_query, preferred_element_type=jnp.float32).reshape(
        half_rows, -1, HD
    )
    queries = rotate(queries, cos_own, sin_own).astype(jnp.bfloat16)
    query_heads = queries.reshape(half_rows, kv_local, -1, HD)
    key_heads = keys.reshape(length, kv_local, HD)
    value_heads = values.reshape(length, kv_local, HD)
    query_idx = base + jnp.arange(half_rows, dtype=jnp.int32)
    key_idx = jnp.arange(length, dtype=jnp.int32)
    offset = query_idx[:, None] - key_idx[None, :]
    allowed = (offset >= 0) & (offset <= own_pos[:, None])
    scores = (
        jnp.einsum("rkgd,lkd->kgrl", query_heads, key_heads, preferred_element_type=jnp.float32)
        * scale
    )
    scores = jnp.where(allowed[None, None], scores, -1e30)
    top = jnp.max(scores, -1, keepdims=True)
    weights = jnp.exp(scores - top)
    probs = weights / jnp.sum(weights, -1, keepdims=True)
    probs_b = probs.astype(jnp.bfloat16)
    attn = jnp.einsum("kgrl,lkd->rkgd", probs_b, value_heads, preferred_element_type=jnp.float32)
    attn = attn.astype(jnp.bfloat16).reshape(half_rows, q_width)
    mixed = lax.psum_scatter(
        jnp.dot(attn, w_out, preferred_element_type=jnp.float32).astype(jnp.bfloat16),
        "tensor",
        scatter_dimension=0,
        tiled=True,
    ).astype(jnp.float32)
    restored = (upper.astype(jnp.float32) - mixed).astype(jnp.bfloat16)
    upstream = lax.all_gather(grad_upper, "tensor", axis=0, tiled=True)
    grad_attn = contract_last(upstream, w_out).astype(jnp.bfloat16)
    out_term = contract_first(attn, upstream)
    grad_out = lax.psum_scatter(
        out_term.astype(jnp.bfloat16), ("dp", "seq"), scatter_dimension=1, tiled=True
    ).astype(jnp.float32)
    grad_heads = grad_attn.reshape(half_rows, kv_local, -1, HD)
    grad_probs = jnp.einsum(
        "rkgd,lkd->kgrl", grad_heads, value_heads, preferred_element_type=jnp.float32
    )
    delta = jnp.sum(probs * grad_probs, -1, keepdims=True)
    grad_scores = (probs * (grad_probs - delta) * scale).astype(jnp.bfloat16)
    grad_q = jnp.einsum(
        "kgrl,lkd->rkgd", grad_scores, key_heads, preferred_element_type=jnp.float32
    ).reshape(half_rows, -1, HD)
    key_terms = jnp.einsum(
        "kgrl,rkgd->lkd", grad_scores, query_heads, preferred_element_type=jnp.float32
    ).reshape(length, -1)
    value_terms = jnp.einsum(
        "kgrl,rkgd->lkd", probs_b, grad_heads, preferred_element_type=jnp.float32
    ).reshape(length, -1)
    key_own, value_own = (
        lax.psum_scatter(
            key_terms.astype(jnp.bfloat16), "seq", scatter_dimension=0, tiled=True
        ).astype(jnp.float32),
        lax.psum_scatter(
            value_terms.astype(jnp.bfloat16), "seq", scatter_dimension=0, tiled=True
        ).astype(jnp.float32),
    )
    grad_query_rows = (
        unrotate(grad_q, cos_own, sin_own).astype(jnp.bfloat16).reshape(half_rows, q_width)
    )
    grad_key_rows = (
        unrotate(key_own.reshape(half_rows, kv_local, HD), cos_own, sin_own)
        .astype(jnp.bfloat16)
        .reshape(half_rows, -1)
    )
    grad_value_rows = value_own.astype(jnp.bfloat16)
    query_term = contract_first(hidden, grad_query_rows)
    key_term = contract_first(hidden, grad_key_rows)
    value_term = contract_first(hidden, grad_value_rows)
    grad_query, grad_key, grad_value = (
        lax.psum_scatter(
            query_term.astype(jnp.bfloat16), ("dp", "seq"), scatter_dimension=0, tiled=True
        ).astype(jnp.float32),
        lax.psum_scatter(
            key_term.astype(jnp.bfloat16), ("dp", "seq"), scatter_dimension=0, tiled=True
        ).astype(jnp.float32),
        lax.psum_scatter(
            value_term.astype(jnp.bfloat16), ("dp", "seq"), scatter_dimension=0, tiled=True
        ).astype(jnp.float32),
    )
    total = contract_last(grad_query_rows, w_query) + contract_last(grad_key_rows, w_key)
    grad_hidden = lax.psum_scatter(
        (total + contract_last(grad_value_rows, w_value)).astype(jnp.bfloat16),
        "tensor",
        scatter_dimension=0,
        tiled=True,
    ).astype(jnp.float32)
    normed_own, inverse_own, hidden_own = norm_rows(lower, norm_gain)
    scaled = norm_gain * grad_hidden
    grad_in = inverse_own * (scaled - normed_own * jnp.mean(scaled * normed_own, -1, keepdims=True))
    grad_lower_in = (grad_lower.astype(jnp.float32) + grad_in).astype(jnp.bfloat16)
    return (restored, grad_lower_in, grad_query, grad_key, grad_value, grad_out)


def solution(mesh):
    in_specs = (
        P(("dp", "seq", "tensor"), None),
        P(("dp", "seq", "tensor"), None),
        P(("dp", "seq", "tensor"), None),
        P(("dp", "seq", "tensor"), None),
        P("dp", None),
        P(),
        P(None, "tensor"),
        P(None, "tensor"),
        P(None, "tensor"),
        P("tensor", None),
    )
    out_specs = (
        P(("dp", "seq", "tensor"), None),
        P(("dp", "seq", "tensor"), None),
        P(("dp", "seq"), "tensor"),
        P(("dp", "seq"), "tensor"),
        P(("dp", "seq"), "tensor"),
        P("tensor", ("dp", "seq")),
    )
    return jax.shard_map(shards, mesh=mesh, in_specs=in_specs, out_specs=out_specs, check_vma=False)
```

profile of v0, /device:TPU:0, one launch (start us, length us, event | category | flops | bytes accessed | tf_op | source)
XLA Modules:
  0.0 602.0 jit_solution(4880508964022735952)
XLA Ops:
  14.0 53.1 %all-gather.5.cloned.1.call-done = bf16[320,4096]{1,0:T(8,128)(2,1)} async-done(((bf16[80,4096]{1,0:T(8,128)(2,1)}), bf16[320,4096]{1,0:T(8,128)(2,1)}) %all-gather.5.cloned.1.call-update) | async-done | bytes 2621456 | tf_op jit(solution)/shard_map/all_gather | solution.py:115
  67.1 7.9 %convolution_convert_fusion.5 = bf16[320,1024]{1,0:T(8,128)(2,1)} fusion(bf16[320,4096]{1,0:T(8,128)(2,1)} %all-gather.5.cloned.1.call-done, bf16[1024,4096]{1,0:T(8,128)(2,1)} %param.19), kind=kOutput, calls=%fused_computation.45 | convolution fusion | flops 2684682240 | bytes 11665408 | tf_op jit(solution)/shard_map/dot_general | solution.py:55
  76.9 77.4 %all-gather.3.cloned.1.call-done = bf16[640,4096]{1,0:T(8,128)(2,1)} async-done(((bf16[80,4096]{1,0:T(8,128)(2,1)}), bf16[640,4096]{1,0:T(8,128)(2,1)}) %all-gather.3.cloned.1.call-update) | async-done | bytes 5242896 | tf_op jit(solution)/shard_map/all_gather | solution.py:81
  154.3 3.7 fusion.2
  158.3 2.1 fusion.4
  160.5 7.4 %fusion.27 = f32[40,8,8,128]{3,1,2,0:T(8,128)S(1)} fusion(bf16[4096,1024]{1,0:T(8,128)(2,1)} %param.16, bf16[640,4096]{1,0:T(8,128)(2,1)S(1)} %fusion.4, s32[]{:T(128)S(6)} %select_n.8), kind=kOutput, calls=%fused_computation.43 | convolution fusion | flops 2684354560 | bytes 12320772 | tf_op jit(solution)/shard_map/dot_general | solution.py:86
  174.7 2.1 copy.81
  176.8 5.0 convolution_convert_fusion.6
  181.8 3.7 fusion.61
  186.6 7.1 %fusion.75 = (f32[2,4,320]{2,1,0:T(4,128)S(1)}, f32[2,4,320,640]{3,2,1,0:T(8,128)}) fusion(pred[320,640]{1,0:T(8,128)(4,1)} %fusion.52, bf16[640,2,64]{2,0,1:T(8,128)(2,1)} %get-tuple-element.9, bf16[640,2,64]{2,0,1:T(8,128)(2,1)} %get-tuple-element.8, bf16[320,2,4,64]{3,0,2,1:T(8,128)(2,1)} %bitcast.125, bf16[320,2,4,64]{3,0,2,1:T(8,128)(2,1)} %bitcast.123), kind=kOutput, calls=%fused_computation.108 | convolution fusion | flops 427950720 | bytes 7751680 | tf_op jit(solution)/shard_map/sub | solution.py:103
  193.6 21.9 %fusion.46 = bf16[2,128,640]{2,1,0:T(8,128)(2,1)} fusion(f32[2,640,320,4]{1,2,3,0:T(8,128)} %fusion.61, bf16[320,2,4,64]{3,0,2,1:T(8,128)(2,1)} %bitcast.126, bf16[320,2,4,64]{3,0,2,1:T(8,128)(2,1)S(1)} %bitcast.124, f32[2,4,320,640]{3,2,1,0:T(8,128)} %get-tuple-element.23, f32[2,4,320]{2,1,0:T(4,128)S(1)} %get-tuple-element.22), kind=kOutput, calls=%fused_computation.61 | convolution fusion | flops 432376960 | bytes 14100480 | tf_op jit(solution)/shard_map/kgrl,rkgd->lkd/dot_general | solution.py:130
  217.5 3.9 fusion.47
  222.4 5.8 reduce-scatter.25.cloned.1.call-done
  230.1 4.4 convolution_convert_fusion.4
  234.5 8.8 %reduce-scatter.27.cloned.1.call-done = bf16[320,256]{1,0:T(8,128)(2,1)} async-done(((bf16[640,256]{1,0:T(8,128)(2,1)}), bf16[320,256]{1,0:T(8,128)(2,1)}) %reduce-scatter.27.cloned.1.call-update) | async-done | bytes 163856
  243.4 4.4 convolution_convert_fusion.3
  247.8 3.9 fusion.39
  252.8 8.2 %convolution_convert_fusion.2 = bf16[320,4096]{1,0:T(8,128)(2,1)} fusion(bf16[320,1024]{1,0:T(8,128)(2,1)S(1)} %reshape.229, bf16[1024,4096]{1,0:T(8,128)(2,1)} %param.19), kind=kOutput, calls=%fused_computation.19 | convolution fusion | flops 2685665280 | bytes 11665408 | tf_op jit(solution)/shard_map/dot_general | solution.py:109
  261.1 22.3 %fusion.15 = f32[2,128,4,320]{1,3,2,0:T(8,128)S(1)} fusion(f32[2,640,320,4]{1,2,3,0:T(8,128)} %fusion.61, bf16[640,2,64]{2,0,1:T(8,128)(2,1)} %get-tuple-element.9, bf16[640,2,64]{2,0,1:T(8,128)(2,1)} %get-tuple-element.8, f32[2,4,320,640]{3,2,1,0:T(8,128)} %get-tuple-element.23, f32[2,4,320]{2,1,0:T(4,128)S(1)} %get-tuple-element.22), kind=kOutput, calls=%fused_computation.29 | convolution fusion | flops 431557760 | bytes 14755840 | tf_op jit(solution)/shard_map/kgrl,lkd->rkgd/dot_general | solution.py:127
  286.5 5.5 fusion.56
  293.5 2.4 fusion.8
  296.0 8.7 %convolution_convert_fusion.1 = bf16[4096,1024]{1,0:T(8,128)(2,1)} fusion(bf16[640,4096]{1,0:T(8,128)(2,1)} %copy-done.3, s32[]{:T(128)S(6)} %select_n.8, bf16[40,8,8,128]{3,2,1,0:T(8,128)(2,1)S(1)} %bitcast.129), kind=kOutput, calls=%fused_computation.8 | convolution fusion | flops 2688548864 | bytes 11665412 | tf_op jit(solution)/shard_map/dot_general | solution.py:61
  305.9 8.7 %convolution_convert_fusion = bf16[1024,4096]{1,0:T(8,128)(2,1)} fusion(bf16[320,1024]{1,0:T(8,128)(2,1)S(1)} %copy-done.17, bf16[320,4096]{1,0:T(8,128)(2,1)} %all-gather.5.cloned.1.call-done), kind=kOutput, calls=%fused_computation.7 | convolution fusion | flops 2688548864 | bytes 11665408 | tf_op jit(solution)/shard_map/dot_general | solution.py:61
  317.7 16.0 %reduce-scatter.21.cloned.1.call-done = bf16[512,256]{1,0:T(8,128)(2,1)} async-done(((bf16[4096,256]{1,0:T(8,128)(2,1)}), bf16[512,256]{1,0:T(8,128)(2,1)}) %reduce-scatter.21.cloned.1.call-update) | async-done | bytes 262160 | tf_op jit(solution)/shard_map/reduce_scatter | solution.py:163
  335.5 52.7 %reduce-scatter.13.cloned.1.call-done = bf16[80,4096]{1,0:T(8,128)(2,1)} async-done(((bf16[320,4096]{1,0:T(8,128)(2,1)}), bf16[80,4096]{1,0:T(8,128)(2,1)}) %reduce-scatter.13.cloned.1.call-update) | async-done | bytes 655376 | tf_op jit(solution)/shard_map/reduce_scatter | solution.py:108
  388.2 2.1 subtract_convert_fusion.1
  390.3 52.0 %reduce-scatter.15.cloned.1.call-done = bf16[80,4096]{1,0:T(8,128)(2,1)} async-done(((bf16[320,4096]{1,0:T(8,128)(2,1)}), bf16[80,4096]{1,0:T(8,128)(2,1)}) %reduce-scatter.15.cloned.1.call-update) | async-done | bytes 655376 | tf_op jit(solution)/shard_map/reduce_scatter | solution.py:168
  443.8 2.6 fusion.37
  446.4 70.4 %reduce-scatter.17.cloned.1.call-done = bf16[512,1024]{1,0:T(8,128)(2,1)} async-done(((bf16[4096,1024]{1,0:T(8,128)(2,1)}), bf16[512,1024]{1,0:T(8,128)(2,1)}) %reduce-scatter.17.cloned.1.call-update) | async-done | bytes 1048592 | tf_op jit(solution)/shard_map/reduce_scatter | solution.py:157
  516.8 2.8 convert_element_type.155
  519.6 72.2 %reduce-scatter.23.cloned.1.call-done = bf16[1024,512]{1,0:T(8,128)(2,1)} async-done(((bf16[1024,4096]{1,0:T(8,128)(2,1)}), bf16[1024,512]{1,0:T(8,128)(2,1)}) %reduce-scatter.23.cloned.1.call-update) | async-done | bytes 1048592 | tf_op jit(solution)/shard_map/reduce_scatter | solution.py:118
  591.8 2.8 convert_element_type.161
  (107 shorter events, 34.7 us)
Async XLA Ops:
  7.2 163.5 %copy-start = (bf16[4096,256]{1,0:T(8,128)(2,1)S(1)}, bf16[4096,256]{1,0:T(8,128)(2,1)}, u32[]{:S(2)}) copy-start(bf16[4096,256]{1,0:T(8,128)(2,1)} %param.17) | copy-start | bytes 6291460
  7.2 59.9 %all-gather.5.cloned.1.call-start = ((), (), s32[]{:S(2)}) async-start(), calls=%async_computation.10 | async-start | bytes 3276800 | tf_op jit(solution)/shard_map/all_gather | solution.py:115
  7.9 146.4 %all-gather.3.cloned.1.call-start = ((), (), s32[]{:S(2)}) async-start(), calls=%async_computation.8 | async-start | bytes 5898240 | tf_op jit(solution)/shard_map/all_gather | solution.py:81
  8.7 219.5 %reduce-scatter.25.cloned.1.call-start = ((), (), s32[]{:S(2)}) async-start(), calls=%async_computation.16 | async-start | bytes 491520
  9.9 65.1 %copy-start.14 = (f32[320,64]{0,1:T(8,128)}, f32[320,64]{0,1:T(8,128)S(1)}, u32[]{:S(2)}) copy-start(f32[320,64]{0,1:T(8,128)S(1)} %get-tuple-element.21) | copy-start | bytes 245764
  10.1 158.1 %copy-start.6 = (f32[320,64]{1,0:T(8,128)}, f32[320,64]{1,0:T(8,128)S(1)}, u32[]{:S(2)}) copy-start(f32[320,64]{1,0:T(8,128)S(1)} %copy.56) | copy-start | bytes 245764
  10.2 158.0 %copy-start.8 = (f32[320,64]{1,0:T(8,128)}, f32[320,64]{1,0:T(8,128)S(1)}, u32[]{:S(2)}) copy-start(f32[320,64]{1,0:T(8,128)S(1)} %copy.57) | copy-start | bytes 245764
  75.0 83.0 %copy-start.23 = (f32[4096]{0:T(1024)S(1)}, f32[4096]{0:T(1024)}, u32[]{:S(2)}) copy-start(f32[4096]{0:T(1024)} %param.15) | copy-start | bytes 49156
  154.3 4.0 copy-start.1
  160.5 10.2 %copy-start.3 = (bf16[640,4096]{1,0:T(8,128)(2,1)}, bf16[640,4096]{1,0:T(8,128)(2,1)S(1)}, u32[]{:S(2)}) copy-start(bf16[640,4096]{1,0:T(8,128)(2,1)S(1)} %fusion.4) | copy-start | bytes 15728644
  181.8 3.8 copy-start.20
  181.8 3.8 copy-start.4
  181.8 3.7 copy-start.10
  181.8 3.7 copy-start.11
  186.6 7.1 %copy-start.18 = (bf16[320,8,64]{2,0,1:T(8,128)(2,1)S(1)}, bf16[320,8,64]{2,0,1:T(8,128)(2,1)}, u32[]{:S(2)}) copy-start(bf16[320,8,64]{2,0,1:T(8,128)(2,1)} %copy.58) | copy-start | bytes 983044
  217.5 11.8 %copy-start.15 = (f32[320,64]{0,1:T(8,128)S(1)}, f32[320,64]{0,1:T(8,128)}, u32[]{:S(2)}) copy-start(f32[320,64]{0,1:T(8,128)} %copy-done.14) | copy-start | bytes 245764
  217.5 25.9 %reduce-scatter.27.cloned.1.call-start = ((), (), s32[]{:S(2)}) async-start(), calls=%async_computation.17 | async-start | bytes 491520
  222.3 93.6 %reduce-scatter.19.cloned.1.call-start = ((), (), s32[]{:S(2)}) async-start(), calls=%async_computation.13 | async-start | bytes 2359296 | tf_op jit(solution)/shard_map/reduce_scatter | solution.py:160
  234.5 13.3 %copy-start.21 = (bf16[640,256]{0,1:T(8,128)(2,1)S(1)}, bf16[640,256]{0,1:T(8,128)(2,1)}, u32[]{:S(2)}) copy-start(bf16[640,256]{0,1:T(8,128)(2,1)} %copy-done.20) | copy-start | bytes 983044
  234.5 99.3 %reduce-scatter.21.cloned.1.call-start = ((), (), s32[]{:S(2)}) async-start(), calls=%async_computation.14 | async-start | bytes 2359296 | tf_op jit(solution)/shard_map/reduce_scatter | solution.py:163
  247.8 140.4 %reduce-scatter.13.cloned.1.call-start = ((), (), s32[]{:S(2)}) async-start(), calls=%async_computation.9 | async-start | bytes 3276800 | tf_op jit(solution)/shard_map/reduce_scatter | solution.py:108
  252.8 8.2 %copy-start.16 = (bf16[320,1024]{1,0:T(8,128)(2,1)}, bf16[320,1024]{1,0:T(8,128)(2,1)S(1)}, u32[]{:S(2)}) copy-start(bf16[320,1024]{1,0:T(8,128)(2,1)S(1)} %reshape.229) | copy-start | bytes 1966084
  261.0 181.3 %reduce-scatter.15.cloned.1.call-start = ((), (), s32[]{:S(2)}) async-start(), calls=%async_computation.11 | async-start | bytes 3276800 | tf_op jit(solution)/shard_map/reduce_scatter | solution.py:168
  283.4 1.0 copy-start.9
  286.4 5.5 copy-start.13
  291.9 1.6 copy-start.5
  291.9 1.6 copy-start.22
  296.0 220.8 %reduce-scatter.17.cloned.1.call-start = ((), (), s32[]{:S(2)}) async-start(), calls=%async_computation.12 | async-start | bytes 9437184 | tf_op jit(solution)/shard_map/reduce_scatter | solution.py:157
  304.8 1.1 copy-start.17
  304.8 287.0 %reduce-scatter.23.cloned.1.call-start = ((), (), s32[]{:S(2)}) async-start(), calls=%async_computation.15 | async-start | bytes 9437184 | tf_op jit(solution)/shard_map/reduce_scatter | solution.py:118
  314.6 1.1 copy-start.2
  314.6 73.6 %copy-start.19 = (bf16[80,4096]{1,0:T(8,128)(2,1)S(1)}, bf16[80,4096]{1,0:T(8,128)(2,1)}, u32[]{:S(2)}) copy-start(bf16[80,4096]{1,0:T(8,128)(2,1)} %param.11) | copy-start | bytes 1966084
  (2 other events, 1.6 us)
Sparse Core Ops, SparseCore 0:
  9.6 57.4 all-gather.4
  69.2 85.0 all-gather.2
  217.6 10.5 reduce-scatter.24
  230.9 12.3 reduce-scatter.26
  247.1 41.3 reduce-scatter.18
  292.5 41.1 reduce-scatter.20
  336.0 52.1 reduce-scatter.12
  390.5 51.7 reduce-scatter.14
  445.8 70.9 reduce-scatter.16
  520.5 71.2 reduce-scatter.22
where the time goes:
time: 610 us; the launch traced here: 602 us
  waiting for transfers between devices  410 us (67%)
  matrix products  129 us (21%)
  other arithmetic  29.4 us (5%)
  local copies, waits for them, and re-layouts  18.4 us (3%)
  between operations  15.1 us (2%)
    all_gather x1, waiting for transfers between devices, shards(): every_row = lax.all_gather(lower, ('seq', 'tensor'), axis=0, tiled=True)  77.4 us
    reduce_scatter x1, waiting for transfers between devices, shards(): lax.psum_scatter(out_term.astype(jnp.bfloat16), ('dp', 'seq'), scatter_di...  72.2 us
    reduce_scatter x1, waiting for transfers between devices, shards(): lax.psum_scatter(query_term.astype(jnp.bfloat16), ('dp', 'seq'), scatter_...  70.4 us
    all_gather x1, waiting for transfers between devices, shards(): upstream = lax.all_gather(grad_upper, 'tensor', axis=0, tiled=True)  53.1 us
    reduce_scatter x1, waiting for transfers between devices, shards(): lax.psum_scatter(jnp.dot(attn, w_out, preferred_element_type=jnp.float32)...  52.7 us
    reduce_scatter x1, waiting for transfers between devices, shards(): lax.psum_scatter((total + contract_last(grad_value_rows, w_value)).astype...  52 us
    dot_general x4, matrix products, contract_first(): lax.dot_general(left, right, (((0,), (0,)), ((), ())), preferred_element_...  26.2 us
    dot_general x1, matrix products, shards(): jnp.einsum('kgrl,lkd->rkgd', grad_scores, key_heads, preferred_element_ty...  22.3 us
  transfers between devices with their start and end apart: 10, of which 9 were waited for; matrix products, arithmetic and copies ran while one was open for 18% of the time, Pallas kernels for 0%

commit v1 on v0

v1 whole, which is shorter than its diff:
```python
import functools
import math

import jax
import jax.numpy as jnp
from jax import lax
from jax.experimental import pallas as pl
from jax.experimental.pallas import tpu as pltpu
from jax.sharding import PartitionSpec as P

HD = 128
F32 = jnp.float32
BF16 = jnp.bfloat16
VMEM_LIMIT = 40 * 1024 * 1024


def tables(positions):
    half = HD // 2
    freq = jnp.exp(jnp.arange(half, dtype=F32) * (-2.0 * math.log(10000.0) / HD))
    angle = positions.astype(F32)[:, None] * freq[None, :]
    cosine, sine = jnp.cos(angle), jnp.sin(angle)
    return jnp.concatenate([cosine, cosine], -1), jnp.concatenate([-sine, sine], -1)


def norm_rows(rows_in, norm_gain):
    rows_f = rows_in.astype(F32)
    inverse = lax.rsqrt(jnp.mean(rows_f * rows_f, -1, keepdims=True) + 1e-05)
    normed = rows_f * inverse
    return (normed, inverse, (normed * norm_gain).astype(BF16))


def contract_last(left, right):
    return lax.dot_general(left, right, (((1,), (1,)), ((), ())), preferred_element_type=F32)


def contract_first(left, right):
    return lax.dot_general(left, right, (((0,), (0,)), ((), ())), preferred_element_type=F32)


def turn(values, cosine, sine):
    return values * cosine + pltpu.roll(values, HD // 2, 1) * sine


def forward_body(q_ref, k_ref, v_ref, cos_ref, sin_ref, qi_ref, ki_ref, pos_ref, rot_ref, probs_ref, attn_ref):
    query = turn(q_ref[...], cos_ref[...], sin_ref[...]).astype(BF16)
    rot_ref[...] = query
    scores = contract_last(query, k_ref[...]) * (HD ** (-0.5))
    offset = qi_ref[...] - ki_ref[...]
    allowed = (offset >= 0) & (offset <= pos_ref[...])
    scores = jnp.where(allowed, scores, -1e30)
    weights = jnp.exp(scores - jnp.max(scores, -1, keepdims=True))
    probs = weights / jnp.sum(weights, -1, keepdims=True)
    probs_ref[0] = probs
    attn_ref[...] = jnp.dot(probs.astype(BF16), v_ref[...], preferred_element_type=F32).astype(BF16)


def backward_body(group, q_ref, k_ref, v_ref, cos_ref, sin_ref, probs_ref, g_ref, dq_ref, dk_ref, dv_ref):
    probs = probs_ref[0]
    grad = g_ref[...]
    grad_probs = contract_last(grad, v_ref[...])
    delta = jnp.sum(probs * grad_probs, -1, keepdims=True)
    grad_scores = (probs * (grad_probs - delta) * (HD ** (-0.5))).astype(BF16)
    grad_q = jnp.dot(grad_scores, k_ref[...], preferred_element_type=F32)
    dq_ref[...] = turn(grad_q, cos_ref[...], -sin_ref[...]).astype(BF16)
    dk = contract_first(grad_scores, q_ref[...])
    dv = contract_first(probs.astype(BF16), grad)
    first = lax.rem(pl.program_id(0), group) == 0

    @pl.when(first)
    def _():
        dk_ref[...] = dk
        dv_ref[...] = dv

    @pl.when(jnp.logical_not(first))
    def _():
        dk_ref[...] += dk
        dv_ref[...] += dv


def attention_specs(rows, length, group):
    head = pl.BlockSpec((rows, HD), lambda h: (0, h))
    shared = pl.BlockSpec((length, HD), lambda h: (0, h // group))
    table = pl.BlockSpec((rows, HD), lambda h: (0, 0))
    column = pl.BlockSpec((rows, 1), lambda h: (0, 0))
    line = pl.BlockSpec((1, length), lambda h: (0, 0))
    square = pl.BlockSpec((1, rows, length), lambda h: (h, 0, 0))
    return head, shared, table, column, line, square


def attention_forward(queries, keys, values, cosine, sine, query_idx, key_idx, positions):
    rows, width = queries.shape
    length = keys.shape[0]
    heads = width // HD
    head, shared, table, column, line, square = attention_specs(rows, length, width // keys.shape[1])
    pairs = heads * rows * length
    return pl.pallas_call(
        forward_body,
        grid=(heads,),
        in_specs=[head, shared, shared, table, table, column, line, column],
        out_specs=[head, square, head],
        out_shape=[
            jax.ShapeDtypeStruct((rows, width), BF16),
            jax.ShapeDtypeStruct((heads, rows, length), F32),
            jax.ShapeDtypeStruct((rows, width), BF16),
        ],
        compiler_params=pltpu.CompilerParams(vmem_limit_bytes=VMEM_LIMIT),
        cost_estimate=pl.CostEstimate(flops=4 * pairs * HD, bytes_accessed=4 * pairs, transcendentals=pairs),
        name="attention_forward",
    )(queries, keys, values, cosine, sine, query_idx[:, None], key_idx[None, :], positions[:, None])


def attention_backward(queries, keys, values, cosine, sine, probs, grads):
    rows, width = queries.shape
    length = keys.shape[0]
    heads = width // HD
    group = width // keys.shape[1]
    head, shared, table, column, line, square = attention_specs(rows, length, group)
    pairs = heads * rows * length
    return pl.pallas_call(
        functools.partial(backward_body, group),
        grid=(heads,),
        in_specs=[head, shared, shared, table, table, square, head],
        out_specs=[head, shared, shared],
        out_shape=[
            jax.ShapeDtypeStruct((rows, width), BF16),
            jax.ShapeDtypeStruct(keys.shape, F32),
            jax.ShapeDtypeStruct(keys.shape, F32),
        ],
        compiler_params=pltpu.CompilerParams(vmem_limit_bytes=VMEM_LIMIT),
        cost_estimate=pl.CostEstimate(flops=8 * pairs * HD, bytes_accessed=4 * pairs, transcendentals=0),
        name="attention_backward",
    )(queries, keys, values, cosine, sine, probs, grads)


def gather_cyclic(block):
    n = lax.axis_size("tensor")
    return [block] + [
        lax.ppermute(block, "tensor", [(i, (i + s) % n) for i in range(n)]) for s in range(1, n)
    ]


def scatter_cyclic(term, rows):
    n = lax.axis_size("tensor")
    total = term[:rows].astype(F32)
    for s in range(1, n):
        part = term[s * rows : (s + 1) * rows]
        total += lax.ppermute(part, "tensor", [(i, (i - s) % n) for i in range(n)]).astype(F32)
    return total


def scatter_groups(term):
    n_dp, n_seq = lax.axis_size("dp"), lax.axis_size("seq")
    dp, seq = lax.axis_index("dp"), lax.axis_index("seq")
    n = n_dp * n_seq
    rows, columns = term.shape[0] // n, term.shape[1]
    blocks = term.reshape(n_dp // 2, 2, n_seq * rows, columns)
    core = dp % 2
    send = lax.dynamic_index_in_dim(blocks, 1 - core, 1, keepdims=False)
    keep = lax.dynamic_index_in_dim(blocks, core, 1, keepdims=False)
    came = lax.ppermute(send, "dp", [(i, i ^ 1) for i in range(n_dp)])
    pair = (keep.astype(F32) + came.astype(F32)).astype(BF16)
    pair = pair.reshape(n // 2, rows, columns)
    mine = (dp // 2) * n_seq + seq
    total = lax.dynamic_index_in_dim(pair, mine, 0, keepdims=False).astype(F32)

    def partner(i, d):
        d_dp, d_seq = d // n_seq, d % n_seq
        i_dp, i_seq = i // n_seq, i % n_seq
        return (i_dp ^ (2 * d_dp)) * n_seq + (i_seq ^ d_seq)

    for d in range(n // 2 - 1, 0, -1):
        part = lax.dynamic_index_in_dim(pair, mine ^ d, 0, keepdims=False)
        total += lax.ppermute(part, ("dp", "seq"), [(i, partner(i, d)) for i in range(n)]).astype(F32)
    return total


def shards(
    lower, upper, grad_upper, grad_lower, positions, norm_gain, w_query, w_key, w_value, w_out
):
    rows = lower.shape[0]
    n_tensor = lax.axis_size("tensor")
    n_seq = lax.axis_size("seq")
    half_rows = rows * n_tensor
    k_width = w_key.shape[1]
    me_t = lax.axis_index("tensor")
    me_s = lax.axis_index("seq")

    lower_blocks = gather_cyclic(lower)
    upstream_blocks = gather_cyclic(grad_upper)

    local = jnp.concatenate(
        [((me_t - s) % n_tensor) * rows + jnp.arange(rows, dtype=jnp.int32) for s in range(n_tensor)]
    )
    own_idx = me_s * half_rows + local
    key_idx = jnp.concatenate([((me_s + e) % n_seq) * half_rows + local for e in range(n_seq)])
    own_pos = jnp.concatenate(
        [
            lax.dynamic_slice_in_dim(
                positions[0], me_s * half_rows + ((me_t - s) % n_tensor) * rows, rows, 0
            )
            for s in range(n_tensor)
        ]
    )
    cosine, sine = tables(own_pos)

    parts = [norm_rows(block, norm_gain) for block in lower_blocks]
    normed_own, inverse_own, _ = parts[0]
    hidden = jnp.concatenate([part[2] for part in parts], 0)

    def rope(values, sine_t):
        heads = values.reshape(half_rows, -1, HD)
        turned = jnp.concatenate([heads[..., HD // 2 :], heads[..., : HD // 2]], -1)
        return (heads * cosine[:, None, :] + turned * sine_t[:, None, :]).reshape(half_rows, -1)

    keys = rope(jnp.dot(hidden, w_key, preferred_element_type=F32), sine).astype(BF16)
    values = jnp.dot(hidden, w_value, preferred_element_type=F32).astype(BF16)
    both = jnp.concatenate([keys, values], 1)
    ring = [both]
    for e in range(1, n_seq):
        ring.append(lax.ppermute(both, "seq", [(i, (i - e) % n_seq) for i in range(n_seq)]))
    ring = jnp.concatenate(ring, 0)
    keys_all, values_all = ring[:, :k_width], ring[:, k_width:]
    queries = jnp.dot(hidden, w_query, preferred_element_type=F32)
    query_rot, probs, attn = attention_forward(
        queries, keys_all, values_all, cosine, sine, own_idx, key_idx, own_pos
    )
    mixed_term = jnp.dot(attn, w_out, preferred_element_type=F32).astype(BF16)
    mixed = scatter_cyclic(mixed_term, rows)
    restored = (upper.astype(F32) - mixed).astype(BF16)

    upstream = jnp.concatenate(upstream_blocks, 0)
    out_term = contract_first(upstream, attn).astype(BF16)
    grad_out = scatter_groups(out_term).T
    grad_attn = contract_last(upstream, w_out).astype(BF16)
    dq, key_terms, value_terms = attention_backward(
        query_rot, keys_all, values_all, cosine, sine, probs, grad_attn
    )
    terms = jnp.concatenate([key_terms, value_terms], 1)
    total = terms[:half_rows]
    for e in range(1, n_seq):
        part = terms[e * half_rows : (e + 1) * half_rows].astype(BF16)
        total += lax.ppermute(part, "seq", [(i, (i + e) % n_seq) for i in range(n_seq)]).astype(F32)
    dk = rope(total[:, :k_width], -sine).astype(BF16)
    dv = total[:, k_width:].astype(BF16)

    query_term = contract_first(hidden, dq).astype(BF16)
    grad_query = scatter_groups(query_term)
    kv_term = contract_first(hidden, jnp.concatenate([dk, dv], 1)).astype(BF16)
    grad_kv = scatter_groups(kv_term)
    grad_key, grad_value = grad_kv[:, :k_width], grad_kv[:, k_width:]

    hidden_term = contract_last(dq, w_query) + contract_last(dk, w_key) + contract_last(dv, w_value)
    grad_hidden = scatter_cyclic(hidden_term.astype(BF16), rows)
    scaled = norm_gain * grad_hidden
    grad_in = inverse_own * (scaled - normed_own * jnp.mean(scaled * normed_own, -1, keepdims=True))
    grad_lower_in = (grad_lower.astype(F32) + grad_in).astype(BF16)
    return (restored, grad_lower_in, grad_query, grad_key, grad_value, grad_out)


def solution(mesh):
    in_specs = (
        P(("dp", "seq", "tensor"), None),
        P(("dp", "seq", "tensor"), None),
        P(("dp", "seq", "tensor"), None),
        P(("dp", "seq", "tensor"), None),
        P("dp", None),
        P(),
        P(None, "tensor"),
        P(None, "tensor"),
        P(None, "tensor"),
        P("tensor", None),
    )
    out_specs = (
        P(("dp", "seq", "tensor"), None),
        P(("dp", "seq", "tensor"), None),
        P(("dp", "seq"), "tensor"),
        P(("dp", "seq"), "tensor"),
        P(("dp", "seq"), "tensor"),
        P("tensor", ("dp", "seq")),
    )
    return jax.shard_map(shards, mesh=mesh, in_specs=in_specs, out_specs=out_specs, check_vma=False)
```

time: 610 us -> 456 us (0.75)
  waiting for transfers between devices: 410 us -> 224 us
  matrix products: 129 us -> 51.4 us
  starting transfers between devices: 0.41 us -> 74.9 us
  local copies, waits for them, and re-layouts: 18.4 us -> 40.1 us
  Pallas kernels: 0 us -> 17 us
  between operations: 15.1 us -> 1.86 us
  other arithmetic: 29.4 us -> 37.6 us
    reduce_scatter x6 -> x0, waiting for transfers between devices: 263 us -> none  [the longest x1 72.2 us: shards(): lax.psum_scatter(out_term.astype(jnp.bfloat16), ('dp', 'seq'), scatter_di...]
    ppermute x0 -> x26, waiting for transfers between devices: none -> 224 us  [the longest x9 83.5 us: scatter_groups(): lax.ppermute(part, ('dp', 'seq'), [(i, partner(i, d)) for i in range(n)])]
    all_gather x2 -> x0, waiting for transfers between devices: 131 us -> none  [the longest x1 77.4 us: shards(): every_row = lax.all_gather(lower, ('seq', 'tensor'), axis=0, tiled=True)]
    ppermute x0 -> x26, starting transfers between devices: none -> 74.9 us  [the longest x6 40.2 us: gather_cyclic(): lax.ppermute(block, 'tensor', [(i, (i + s) % n) for i in range(n)])]
    dot_general x9 -> x4, matrix products: 78.4 us -> 17.5 us  [the longest x1 7.62 us: shards(): mixed_term = jnp.dot(attn, w_out, preferred_element_type=F32).astype(BF16)]
    pallas_call x0 -> x2, Pallas kernels: none -> 17 us  [the longest x1 8.8 us: attention_backward(): pl.pallas_call(functools.partial(backward_body, group), grid=(heads,), in...]
    unnamed x12 -> x0, waiting for transfers between devices: 16.1 us -> none
    squeeze x0 -> x6, local copies, waits for them, and re-layouts: none -> 11.3 us  [the longest x3 7.24 us: scatter_groups(): send = lax.dynamic_index_in_dim(blocks, 1 - core, 1, keepdims=False)]
  transfers between devices with their start and end apart: 10 -> 26, of which waited for: 9 -> 11; matrix products, arithmetic and copies ran while one was open for 18% -> 19% of each run, Pallas kernels for 0% -> 0%
where the time goes in v1:
time: 456 us; the launch traced here: 447 us
  waiting for transfers between devices  224 us (49%)
  starting transfers between devices  74.9 us (16%)
  matrix products  51.4 us (11%)
  local copies, waits for them, and re-layouts  40.1 us (9%)
  other arithmetic  37.6 us (8%)
  Pallas kernels  17 us (4%)
    ppermute x9, waiting for transfers between devices, scatter_groups(): lax.ppermute(part, ('dp', 'seq'), [(i, partner(i, d)) for i in range(n)])  83.5 us
    ppermute x6, waiting for transfers between devices, gather_cyclic(): lax.ppermute(block, 'tensor', [(i, (i + s) % n) for i in range(n)])  71.5 us
    ppermute x6, waiting for transfers between devices, scatter_cyclic(): lax.ppermute(part, 'tensor', [(i, (i - s) % n) for i in range(n)])  69.3 us
    ppermute x6, starting transfers between devices, gather_cyclic(): lax.ppermute(block, 'tensor', [(i, (i + s) % n) for i in range(n)])  40.2 us
    ppermute x6, starting transfers between devices, scatter_cyclic(): lax.ppermute(part, 'tensor', [(i, (i - s) % n) for i in range(n)])  20.5 us
    dot_general x4, matrix products, contract_last(): lax.dot_general(left, right, (((1,), (1,)), ((), ())), preferred_element_...  18.2 us
    dot_general x3, matrix products, contract_first(): lax.dot_general(left, right, (((0,), (0,)), ((), ())), preferred_element_...  15.6 us
    unnamed x77, local copies, waits for them, and re-layouts  14.9 us
  transfers between devices with their start and end apart: 26, of which 11 were waited for; matrix products, arithmetic and copies ran while one was open for 19% of the time, Pallas kernels for 0%

profile of v1, /device:TPU:0, one launch (start us, length us, event | category | flops | bytes accessed | tf_op | source)
XLA Modules:
  0.0 447.1 jit_solution(5858879260819936711)
XLA Ops:
  0.7 4.1 collective-permute-start.8
  8.6 3.8 collective-permute-start.2
  19.0 45.2 %collective-permute-done = bf16[80,4096]{1,0:T(8,128)(2,1)} collective-permute-done((bf16[80,4096]{1,0:T(8,128)(2,1)}, bf16[80,4096]{1,0:T(8,128)(2,1)}, u32[]{:S(2)}, u32[]{:S(2)}) %collective-permute-start) | collective-permute-done | bytes 655392 | tf_op jit(solution)/shard_map/ppermute | solution.py:138
  64.2 28.5 %collective-permute-start.1 = (bf16[80,4096]{1,0:T(8,128)(2,1)S(1)}, bf16[80,4096]{1,0:T(8,128)(2,1)S(1)}, u32[]{:S(2)}, u32[]{:S(2)}) collective-permute-start(bf16[80,4096]{1,0:T(8,128)(2,1)S(1)} %copy-done.4), channel_id=1, source_target_pairs={{0,2},{1,3},{2,0},{3,1},{4,6},{5,7},{6,4},{7,5},{8,10},{9,11},{10,... | collective-permute-start | bytes 1966088 | tf_op jit(solution)/shard_map/ppermute | solution.py:138
  95.4 26.3 %collective-permute-done.1 = bf16[80,4096]{1,0:T(8,128)(2,1)S(1)} collective-permute-done((bf16[80,4096]{1,0:T(8,128)(2,1)S(1)}, bf16[80,4096]{1,0:T(8,128)(2,1)S(1)}, u32[]{:S(2)}, u32[]{:S(2)}) %collective-permute-start.1) | collective-permute-done | bytes 655392 | tf_op jit(solution)/shard_map/ppermute | solution.py:138
  133.7 6.8 %fusion.47.q_ref = f32[320,1024]{1,0:T(8,128)S(1)} fusion(bf16[4096,1024]{1,0:T(8,128)(2,1)} %param.16, bf16[80,4096]{1,0:T(8,128)(2,1)S(1)} %copy-done.24, bf16[80,4096]{1,0:T(8,128)(2,1)S(1)} %copy-done.21, bf16[80,4096]{1,0:T(8,128)(2,1)S(1)} %copy-done.18, bf16[80,4096]{1,0:T(8,128)(2,1)S(1)} %copy-done.15), kind=kOutput, calls=%fused_computation.126 | convolution fusion | flops 2694840320 | bytes 12320768 | tf_op jit(solution)/shard_map/dot_general | solution.py:223
  144.0 2.9 convolution_convert_fusion.4.g_ref
  147.0 8.2 %attention_forward.1 = (bf16[320,1024]{1,0:T(8,128)(2,1)S(1)}, f32[8,320,640]{2,1,0:T(8,128)S(1)}, bf16[320,1024]{1,0:T(8,128)(2,1)S(1)}) custom-call(f32[320,1024]{1,0:T(8,128)S(1)} %fusion.47.q_ref, bf16[640,256]{1,0:T(8,128)(2,1)S(1)} %get-tuple-element.56.k_ref, bf16[640,256]{1,0:T(8,128)(2,1)S(1)} %get-tuple-element.55.v_ref, ...), custom_call_target="tpu_custom_call" | custom-call | flops 838860800 | bytes 6553600 | tf_op jit(solution)/shard_map/attention_forward/pallas_call | solution.py:96
  155.3 7.6 %convolution_convert_fusion.3 = bf16[320,4096]{1,0:T(8,128)(2,1)} fusion(bf16[320,1024]{1,0:T(8,128)(2,1)S(1)} %get-tuple-element.12, bf16[1024,4096]{1,0:T(8,128)(2,1)} %param.19), kind=kOutput, calls=%fused_computation.10 | convolution fusion | flops 2685665280 | bytes 11665408 | tf_op jit(solution)/shard_map/dot_general | solution.py:227
  162.9 6.7 %convolution_convert_fusion = bf16[4096,1024]{1,0:T(8,128)(2,1)} fusion(bf16[320,4096]{1,0:T(8,128)(2,1)S(1)} %constant_dynamic-update-slice_fusion, bf16[320,1024]{1,0:T(8,128)(2,1)S(1)} %get-tuple-element.12), kind=kOutput, calls=%fused_computation.4 | convolution fusion | flops 2688548864 | bytes 11665408 | tf_op jit(solution)/shard_map/dot_general | solution.py:37
  169.6 8.8 %attention_backward.1 = (bf16[320,1024]{1,0:T(8,128)(2,1)S(1)}, f32[640,256]{1,0:T(8,128)S(1)}, f32[640,256]{1,0:T(8,128)S(1)}) custom-call(bf16[320,1024]{1,0:T(8,128)(2,1)S(1)} %get-tuple-element.13.q_ref, bf16[640,256]{1,0:T(8,128)(2,1)S(1)} %get-tuple-element.56.k_ref, bf16[640,256]{1,0:T(8,128)(2,1)S(1)} %get-tuple-element.55.v_ref, ...), custom_call_target="tpu_custom_call" | custom-call | flops 1677721600 | bytes 6553600 | tf_op jit(solution)/shard_map/attention_backward/pallas_call | solution.py:119
  178.5 10.9 %fusion.56 = f32[320,4096]{1,0:T(8,128)} fusion(bf16[320,1024]{1,0:T(8,128)(2,1)S(1)} %get-tuple-element.15, bf16[4096,1024]{1,0:T(8,128)(2,1)} %param.16), kind=kOutput, calls=%fused_computation.135 | convolution fusion | flops 2684354560 | bytes 14286848 | tf_op jit(solution)/shard_map/dot_general | solution.py:33
  189.4 4.8 %convolution_convert_fusion.1 = bf16[4096,1024]{1,0:T(8,128)(2,1)S(1)} fusion(bf16[320,1024]{1,0:T(8,128)(2,1)S(1)} %get-tuple-element.15, bf16[80,4096]{1,0:T(8,128)(2,1)S(1)} %copy-done.25, bf16[80,4096]{1,0:T(8,128)(2,1)S(1)} %copy-done.22, bf16[80,4096]{1,0:T(8,128)(2,1)S(1)} %copy-done.19, bf16[80,4096]{1,0:T(8,128)(2,1)S(1)} %copy-done.16), kind=kOutput, calls=%fused_computation.5 | convolution fusion | flops 2699034624 | bytes 11665408 | tf_op jit(solution)/shard_map/dot_general | solution.py:37
  201.5 4.6 %dynamic-slice_bitcast_fusion = bf16[2,1024,1024]{2,1,0:T(8,128)(2,1)} fusion(bf16[2,2,1024,1024]{3,2,1,0:T(8,128)(2,1)} %bitcast.109, s32[]{:T(128)S(6)} %select_n.107), kind=kLoop, calls=%fused_computation.13 | loop fusion | bytes 8388612 | tf_op jit(solution)/shard_map/jit(dynamic_index_in_dim)/squeeze | solution.py:158
  215.4 3.5 convolution_add_fusion.1
  222.6 8.7 %collective-permute-done.4 = bf16[80,4096]{1,0:T(8,128)(2,1)} collective-permute-done((bf16[80,4096]{1,0:T(8,128)(2,1)}, bf16[80,4096]{1,0:T(8,128)(2,1)}, u32[]{:S(2)}, u32[]{:S(2)}) %collective-permute-start.4) | collective-permute-done | bytes 655392 | tf_op jit(solution)/shard_map/ppermute | solution.py:147
  231.4 4.1 convolution_convert_fusion.2
  235.8 21.1 %collective-permute-done.5 = bf16[80,4096]{1,0:T(8,128)(2,1)} collective-permute-done((bf16[80,4096]{1,0:T(8,128)(2,1)}, bf16[80,4096]{1,0:T(8,128)(2,1)}, u32[]{:S(2)}, u32[]{:S(2)}) %collective-permute-start.5) | collective-permute-done | bytes 655392 | tf_op jit(solution)/shard_map/ppermute | solution.py:147
  256.9 14.9 %collective-permute-start.13 = (bf16[80,4096]{1,0:T(8,128)(2,1)S(1)}, bf16[80,4096]{1,0:T(8,128)(2,1)S(1)}, u32[]{:S(2)}, u32[]{:S(2)}) collective-permute-start(bf16[80,4096]{1,0:T(8,128)(2,1)S(1)} %copy-done.29), channel_id=1, source_target_pairs={{0,1},{1,2},{2,3},{3,0},{4,5},{5,6},{6,7},{7,4},{8,9},{9,10},{10,1... | collective-permute-start | bytes 1966088 | tf_op jit(solution)/shard_map/ppermute | solution.py:147
  271.7 3.4 collective-permute-start.12
  275.1 3.0 subtract_convert_fusion
  278.1 12.1 %collective-permute-done.13 = bf16[80,4096]{1,0:T(8,128)(2,1)S(1)} collective-permute-done((bf16[80,4096]{1,0:T(8,128)(2,1)S(1)}, bf16[80,4096]{1,0:T(8,128)(2,1)S(1)}, u32[]{:S(2)}, u32[]{:S(2)}) %collective-permute-start.13) | collective-permute-done | bytes 655392 | tf_op jit(solution)/shard_map/ppermute | solution.py:147
  290.2 27.4 %collective-permute-done.12 = bf16[80,4096]{1,0:T(8,128)(2,1)S(1)} collective-permute-done((bf16[80,4096]{1,0:T(8,128)(2,1)S(1)}, bf16[80,4096]{1,0:T(8,128)(2,1)S(1)}, u32[]{:S(2)}, u32[]{:S(2)}) %collective-permute-start.12) | collective-permute-done | bytes 655392 | tf_op jit(solution)/shard_map/ppermute | solution.py:147
  319.3 5.6 %fusion = bf16[2,1024,1024]{2,1,0:T(8,128)(2,1)S(1)} fusion(bf16[2,1024,1024]{2,1,0:T(8,128)(2,1)} %collective-permute-done.22, bf16[2,2,1024,1024]{3,2,1,0:T(8,128)(2,1)} %bitcast.110, s32[]{:T(128)S(6)} %select_n.106), kind=kLoop, calls=%fused_computation.1 | loop fusion | flops 8388608 | bytes 12582916 | tf_op jit(solution)/shard_map/convert_element_type | solution.py:161
  334.3 5.6 %fusion.1 = bf16[2,1024,1024]{2,1,0:T(8,128)(2,1)S(1)} fusion(bf16[2,1024,1024]{2,1,0:T(8,128)(2,1)} %collective-permute-done.14, bf16[2,2,1024,1024]{3,2,1,0:T(8,128)(2,1)} %bitcast.108, s32[]{:T(128)S(6)} %select_n.106), kind=kLoop, calls=%fused_computation.3 | loop fusion | flops 8388608 | bytes 12582916 | tf_op jit(solution)/shard_map/convert_element_type | solution.py:161
  342.9 21.7 %collective-permute-done.19 = bf16[512,512]{1,0:T(8,128)(2,1)S(1)} collective-permute-done((bf16[512,512]{1,0:T(8,128)(2,1)S(1)}, bf16[512,512]{1,0:T(8,128)(2,1)S(1)}, u32[]{:S(2)}, u32[]{:S(2)}) %collective-permute-start.19) | collective-permute-done | bytes 524320 | tf_op jit(solution)/shard_map/ppermute | solution.py:173
  366.8 8.2 %collective-permute-done.21 = bf16[512,512]{1,0:T(8,128)(2,1)} collective-permute-done((bf16[512,512]{1,0:T(8,128)(2,1)}, bf16[512,512]{1,0:T(8,128)(2,1)}, u32[]{:S(2)}, u32[]{:S(2)}) %collective-permute-start.21) | collective-permute-done | bytes 524320 | tf_op jit(solution)/shard_map/ppermute | solution.py:173
  383.7 14.6 %collective-permute-done.25 = bf16[512,1024]{1,0:T(8,128)(2,1)S(1)} collective-permute-done((bf16[512,1024]{1,0:T(8,128)(2,1)S(1)}, bf16[512,1024]{1,0:T(8,128)(2,1)S(1)}, u32[]{:S(2)}, u32[]{:S(2)}) %collective-permute-start.25) | collective-permute-done | bytes 1048608 | tf_op jit(solution)/shard_map/ppermute | solution.py:173
  400.5 2.9 copy.35
  403.4 17.5 %collective-permute-done.15 = bf16[512,1024]{1,0:T(8,128)(2,1)} collective-permute-done((bf16[512,1024]{1,0:T(8,128)(2,1)}, bf16[512,1024]{1,0:T(8,128)(2,1)}, u32[]{:S(2)}, u32[]{:S(2)}) %collective-permute-start.15) | collective-permute-done | bytes 1048608 | tf_op jit(solution)/shard_map/ppermute | solution.py:173
  420.9 21.4 %collective-permute-done.17 = bf16[512,1024]{1,0:T(8,128)(2,1)} collective-permute-done((bf16[512,1024]{1,0:T(8,128)(2,1)}, bf16[512,1024]{1,0:T(8,128)(2,1)}, u32[]{:S(2)}, u32[]{:S(2)}) %collective-permute-start.17) | collective-permute-done | bytes 1048608 | tf_op jit(solution)/shard_map/ppermute | solution.py:173
  442.3 4.3 fusion.8
  (174 shorter events, 76.1 us)
Async XLA Ops:
  0.6 125.1 %copy-start = (bf16[4096,256]{1,0:T(8,128)(2,1)S(1)}, bf16[4096,256]{1,0:T(8,128)(2,1)}, u32[]{:S(2)}) copy-start(bf16[4096,256]{1,0:T(8,128)(2,1)} %param.17) | copy-start | bytes 6291460
  0.6 63.6 %copy-start.4 = (bf16[80,4096]{1,0:T(8,128)(2,1)S(1)}, bf16[80,4096]{1,0:T(8,128)(2,1)}, u32[]{:S(2)}) copy-start(bf16[80,4096]{1,0:T(8,128)(2,1)} %param.10) | copy-start | bytes 1966084
  0.7 141.0 %collective-permute-start.8 = (bf16[80,4096]{1,0:T(8,128)(2,1)}, bf16[80,4096]{1,0:T(8,128)(2,1)}, u32[]{:S(2)}, u32[]{:S(2)}) collective-permute-start(bf16[80,4096]{1,0:T(8,128)(2,1)} %param.12), channel_id=1, source_target_pairs={{0,2},{1,3},{2,0},{3,1},{4,6},{5,7},{6,4},{7,5},{8,10},{9,11},{10,... | collective-permute-start | bytes 1966088 | tf_op jit(solution)/shard_map/ppermute | solution.py:138
  4.8 135.8 %collective-permute-start.7 = (bf16[80,4096]{1,0:T(8,128)(2,1)}, bf16[80,4096]{1,0:T(8,128)(2,1)}, u32[]{:S(2)}, u32[]{:S(2)}) collective-permute-start(bf16[80,4096]{1,0:T(8,128)(2,1)} %param.12), channel_id=1, source_target_pairs={{0,1},{1,2},{2,3},{3,0},{4,5},{5,6},{6,7},{7,4},{8,9},{9,10},{10,1... | collective-permute-start | bytes 1966088 | tf_op jit(solution)/shard_map/ppermute | solution.py:138
  6.3 136.5 %collective-permute-start.9 = (bf16[80,4096]{1,0:T(8,128)(2,1)}, bf16[80,4096]{1,0:T(8,128)(2,1)}, u32[]{:S(2)}, u32[]{:S(2)}) collective-permute-start(bf16[80,4096]{1,0:T(8,128)(2,1)} %param.12), channel_id=1, source_target_pairs={{0,3},{1,0},{2,1},{3,2},{4,7},{5,4},{6,5},{7,6},{8,11},{9,8},{10,9... | collective-permute-start | bytes 1966088 | tf_op jit(solution)/shard_map/ppermute | solution.py:138
  8.6 55.7 %collective-permute-start = (bf16[80,4096]{1,0:T(8,128)(2,1)}, bf16[80,4096]{1,0:T(8,128)(2,1)}, u32[]{:S(2)}, u32[]{:S(2)}) collective-permute-start(bf16[80,4096]{1,0:T(8,128)(2,1)} %param.10), channel_id=1, source_target_pairs={{0,1},{1,2},{2,3},{3,0},{4,5},{5,6},{6,7},{7,4},{8,9},{9,10},{10,1... | collective-permute-start | bytes 1966088 | tf_op jit(solution)/shard_map/ppermute | solution.py:138
  8.6 85.5 %collective-permute-start.2 = (bf16[80,4096]{1,0:T(8,128)(2,1)}, bf16[80,4096]{1,0:T(8,128)(2,1)}, u32[]{:S(2)}, u32[]{:S(2)}) collective-permute-start(bf16[80,4096]{1,0:T(8,128)(2,1)} %param.10), channel_id=1, source_target_pairs={{0,3},{1,0},{2,1},{3,2},{4,7},{5,4},{6,5},{7,6},{8,11},{9,8},{10,9... | collective-permute-start | bytes 1966088 | tf_op jit(solution)/shard_map/ppermute | solution.py:138
  14.1 107.8 %copy-start.33 = (f32[4096]{0:T(1024)S(1)}, f32[4096]{0:T(1024)}, u32[]{:S(2)}) copy-start(f32[4096]{0:T(1024)} %param.15) | copy-start | bytes 49156
  64.2 57.4 %collective-permute-start.1 = (bf16[80,4096]{1,0:T(8,128)(2,1)S(1)}, bf16[80,4096]{1,0:T(8,128)(2,1)S(1)}, u32[]{:S(2)}, u32[]{:S(2)}) collective-permute-start(bf16[80,4096]{1,0:T(8,128)(2,1)S(1)} %copy-done.4), channel_id=1, source_target_pairs={{0,2},{1,3},{2,0},{3,1},{4,6},{5,7},{6,4},{7,5},{8,10},{9,11},{10,... | collective-permute-start | bytes 1966088 | tf_op jit(solution)/shard_map/ppermute | solution.py:138
  132.2 14.7 %collective-permute-start.3 = (bf16[320,512]{1,0:T(8,128)(2,1)S(1)}, bf16[320,512]{1,0:T(8,128)(2,1)S(1)}, u32[]{:S(2)}, u32[]{:S(2)}) collective-permute-start(bf16[320,512]{1,0:T(8,128)(2,1)S(1)} %pad_maximum_fusion.2), channel_id=1, source_target_pairs={{0,4},{4,0},{1,5},{5,1},{2,6},{6,2},{3,7},{7,3},{8,12},{12,8},{9,1... | collective-permute-start | bytes 983048 | tf_op jit(solution)/shard_map/ppermute | solution.py:220
  194.5 14.1 %collective-permute-start.10 = (bf16[320,512]{1,0:T(8,128)(2,1)S(1)}, bf16[320,512]{1,0:T(8,128)(2,1)S(1)}, u32[]{:S(2)}, u32[]{:S(2)}) collective-permute-start(bf16[320,512]{1,0:T(8,128)(2,1)S(1)} %slice.112), channel_id=1, source_target_pairs={{0,4},{4,0},{1,5},{5,1},{2,6},{6,2},{3,7},{7,3},{8,12},{12,8},{9,1... | collective-permute-start | bytes 983048 | tf_op jit(solution)/shard_map/ppermute | solution.py:242
  199.3 32.1 %collective-permute-start.4 = (bf16[80,4096]{1,0:T(8,128)(2,1)}, bf16[80,4096]{1,0:T(8,128)(2,1)}, u32[]{:S(2)}, u32[]{:S(2)}) collective-permute-start(bf16[80,4096]{1,0:T(8,128)(2,1)} %get-tuple-element.47), channel_id=1, source_target_pairs={{0,3},{1,0},{2,1},{3,2},{4,7},{5,4},{6,5},{7,6},{8,11},{9,8},{10,9... | collective-permute-start | bytes 1966088 | tf_op jit(solution)/shard_map/ppermute | solution.py:147
  199.7 36.0 %collective-permute-start.6 = (bf16[80,4096]{1,0:T(8,128)(2,1)}, bf16[80,4096]{1,0:T(8,128)(2,1)}, u32[]{:S(2)}, u32[]{:S(2)}) collective-permute-start(bf16[80,4096]{1,0:T(8,128)(2,1)} %get-tuple-element.48), channel_id=1, source_target_pairs={{0,1},{1,2},{2,3},{3,0},{4,5},{5,6},{6,7},{7,4},{8,9},{9,10},{10,1... | collective-permute-start | bytes 1966088 | tf_op jit(solution)/shard_map/ppermute | solution.py:147
  201.5 55.4 %collective-permute-start.5 = (bf16[80,4096]{1,0:T(8,128)(2,1)}, bf16[80,4096]{1,0:T(8,128)(2,1)}, u32[]{:S(2)}, u32[]{:S(2)}) collective-permute-start(bf16[80,4096]{1,0:T(8,128)(2,1)} %get-tuple-element.49), channel_id=1, source_target_pairs={{0,2},{1,3},{2,0},{3,1},{4,6},{5,7},{6,4},{7,5},{8,10},{9,11},{10,... | collective-permute-start | bytes 1966088 | tf_op jit(solution)/shard_map/ppermute | solution.py:147
  206.1 113.2 %collective-permute-start.22 = (bf16[2,1024,1024]{2,1,0:T(8,128)(2,1)}, bf16[2,1024,1024]{2,1,0:T(8,128)(2,1)}, u32[]{:S(2)}, u32[]{:S(2)}) collective-permute-start(bf16[2,1024,1024]{2,1,0:T(8,128)(2,1)} %dynamic-slice_bitcast_fusion), channel_id=1, source_target_pairs={{0,8},{8,0},{16,24},{24,16},{1,9},{9,1},{17,25},{25,17},{2,10},{10... | collective-permute-start | bytes 12582920 | tf_op jit(solution)/shard_map/ppermute | solution.py:160
  208.6 123.9 %collective-permute-start.14 = (bf16[2,1024,1024]{2,1,0:T(8,128)(2,1)}, bf16[2,1024,1024]{2,1,0:T(8,128)(2,1)}, u32[]{:S(2)}, u32[]{:S(2)}) collective-permute-start(bf16[2,1024,1024]{2,1,0:T(8,128)(2,1)} %dynamic-slice_bitcast_fusion.1), channel_id=1, source_target_pairs={{0,8},{8,0},{16,24},{24,16},{1,9},{9,1},{17,25},{25,17},{2,10},{10... | collective-permute-start | bytes 12582920 | tf_op jit(solution)/shard_map/ppermute | solution.py:160
  231.4 40.4 %collective-permute-start.11 = (bf16[80,4096]{1,0:T(8,128)(2,1)}, bf16[80,4096]{1,0:T(8,128)(2,1)}, u32[]{:S(2)}, u32[]{:S(2)}) collective-permute-start(bf16[80,4096]{1,0:T(8,128)(2,1)} %get-tuple-element.44), channel_id=1, source_target_pairs={{0,3},{1,0},{2,1},{3,2},{4,7},{5,4},{6,5},{7,6},{8,11},{9,8},{10,9... | collective-permute-start | bytes 1966088 | tf_op jit(solution)/shard_map/ppermute | solution.py:147
  235.5 39.6 %copy-start.27 = (bf16[80,4096]{1,0:T(8,128)(2,1)S(1)}, bf16[80,4096]{1,0:T(8,128)(2,1)}, u32[]{:S(2)}) copy-start(bf16[80,4096]{1,0:T(8,128)(2,1)} %param.11) | copy-start | bytes 1966084
  235.7 81.9 %copy-start.3 = (bf16[320,4096]{1,0:T(8,128)(2,1)S(1)}, bf16[320,4096]{1,0:T(8,128)(2,1)}, u32[]{:S(2)}) copy-start(bf16[320,4096]{1,0:T(8,128)(2,1)} %copy-done.2) | copy-start | bytes 7864324
  235.7 91.6 %collective-permute-start.18 = (bf16[2,1024,512]{2,1,0:T(8,128)(2,1)S(1)}, bf16[2,1024,512]{2,1,0:T(8,128)(2,1)S(1)}, u32[]{:S(2)}, u32[]{:S(2)}) collective-permute-start(bf16[2,1024,512]{2,1,0:T(8,128)(2,1)S(1)} %dynamic-slice_bitcast_fusion.2), channel_id=1, source_target_pairs={{0,8},{8,0},{16,24},{24,16},{1,9},{9,1},{17,25},{25,17},{2,10},{10... | collective-permute-start | bytes 6291464 | tf_op jit(solution)/shard_map/ppermute | solution.py:160
  256.9 33.3 %collective-permute-start.13 = (bf16[80,4096]{1,0:T(8,128)(2,1)S(1)}, bf16[80,4096]{1,0:T(8,128)(2,1)S(1)}, u32[]{:S(2)}, u32[]{:S(2)}) collective-permute-start(bf16[80,4096]{1,0:T(8,128)(2,1)S(1)} %copy-done.29), channel_id=1, source_target_pairs={{0,1},{1,2},{2,3},{3,0},{4,5},{5,6},{6,7},{7,4},{8,9},{9,10},{10,1... | collective-permute-start | bytes 1966088 | tf_op jit(solution)/shard_map/ppermute | solution.py:147
  271.7 45.8 %collective-permute-start.12 = (bf16[80,4096]{1,0:T(8,128)(2,1)S(1)}, bf16[80,4096]{1,0:T(8,128)(2,1)S(1)}, u32[]{:S(2)}, u32[]{:S(2)}) collective-permute-start(bf16[80,4096]{1,0:T(8,128)(2,1)S(1)} %copy-done.28), channel_id=1, source_target_pairs={{0,2},{1,3},{2,0},{3,1},{4,6},{5,7},{6,4},{7,5},{8,10},{9,11},{10,... | collective-permute-start | bytes 1966088 | tf_op jit(solution)/shard_map/ppermute | solution.py:147
  326.1 51.8 %collective-permute-start.23 = (bf16[512,1024]{1,0:T(8,128)(2,1)}, bf16[512,1024]{1,0:T(8,128)(2,1)S(1)}, u32[]{:S(2)}, u32[]{:S(2)}) collective-permute-start(bf16[512,1024]{1,0:T(8,128)(2,1)} %get-tuple-element.38), channel_id=1, source_target_pairs={{0,20},{4,16},{8,28},{12,24},{16,4},{20,0},{24,12},{28,8},{1,21},{... | collective-permute-start | bytes 3145736 | tf_op jit(solution)/shard_map/ppermute | solution.py:173
  329.0 35.5 %collective-permute-start.19 = (bf16[512,512]{1,0:T(8,128)(2,1)S(1)}, bf16[512,512]{1,0:T(8,128)(2,1)S(1)}, u32[]{:S(2)}, u32[]{:S(2)}) collective-permute-start(bf16[512,512]{1,0:T(8,128)(2,1)S(1)} %get-tuple-element.50), channel_id=1, source_target_pairs={{0,20},{4,16},{8,28},{12,24},{16,4},{20,0},{24,12},{28,8},{1,21},{... | collective-permute-start | bytes 1572872 | tf_op jit(solution)/shard_map/ppermute | solution.py:173
  330.8 44.2 %collective-permute-start.21 = (bf16[512,512]{1,0:T(8,128)(2,1)}, bf16[512,512]{1,0:T(8,128)(2,1)}, u32[]{:S(2)}, u32[]{:S(2)}) collective-permute-start(bf16[512,512]{1,0:T(8,128)(2,1)} %get-tuple-element.51), channel_id=1, source_target_pairs={{0,4},{4,0},{8,12},{12,8},{16,20},{20,16},{24,28},{28,24},{1,5},{5... | collective-permute-start | bytes 1572872 | tf_op jit(solution)/shard_map/ppermute | solution.py:173
  331.0 45.1 %collective-permute-start.20 = (bf16[512,512]{1,0:T(8,128)(2,1)}, bf16[512,512]{1,0:T(8,128)(2,1)}, u32[]{:S(2)}, u32[]{:S(2)}) collective-permute-start(bf16[512,512]{1,0:T(8,128)(2,1)} %get-tuple-element.52), channel_id=1, source_target_pairs={{0,16},{4,20},{8,24},{12,28},{16,0},{20,4},{24,8},{28,12},{1,17},{... | collective-permute-start | bytes 1572872 | tf_op jit(solution)/shard_map/ppermute | solution.py:173
  332.5 65.8 %collective-permute-start.25 = (bf16[512,1024]{1,0:T(8,128)(2,1)S(1)}, bf16[512,1024]{1,0:T(8,128)(2,1)S(1)}, u32[]{:S(2)}, u32[]{:S(2)}) collective-permute-start(bf16[512,1024]{1,0:T(8,128)(2,1)S(1)} %get-tuple-element.39), channel_id=1, source_target_pairs={{0,4},{4,0},{8,12},{12,8},{16,20},{20,16},{24,28},{28,24},{1,5},{5... | collective-permute-start | bytes 3145736 | tf_op jit(solution)/shard_map/ppermute | solution.py:173
  339.9 38.6 %copy-start.13 = (bf16[80,4096]{1,0:T(8,128)(2,1)S(1)}, bf16[80,4096]{1,0:T(8,128)(2,1)}, u32[]{:S(2)}) copy-start(bf16[80,4096]{1,0:T(8,128)(2,1)} %param.13) | copy-start | bytes 1966084
  365.3 33.0 %collective-permute-start.24 = (bf16[512,1024]{1,0:T(8,128)(2,1)S(1)}, bf16[512,1024]{1,0:T(8,128)(2,1)S(1)}, u32[]{:S(2)}, u32[]{:S(2)}) collective-permute-start(bf16[512,1024]{1,0:T(8,128)(2,1)S(1)} %get-tuple-element.40), channel_id=1, source_target_pairs={{0,16},{4,20},{8,24},{12,28},{16,0},{20,4},{24,8},{28,12},{1,17},{... | collective-permute-start | bytes 3145736 | tf_op jit(solution)/shard_map/ppermute | solution.py:173
  375.0 45.9 %collective-permute-start.15 = (bf16[512,1024]{1,0:T(8,128)(2,1)}, bf16[512,1024]{1,0:T(8,128)(2,1)}, u32[]{:S(2)}, u32[]{:S(2)}) collective-permute-start(bf16[512,1024]{1,0:T(8,128)(2,1)} %get-tuple-element.41), channel_id=1, source_target_pairs={{0,20},{4,16},{8,28},{12,24},{16,4},{20,0},{24,12},{28,8},{1,21},{... | collective-permute-start | bytes 3145736 | tf_op jit(solution)/shard_map/ppermute | solution.py:173
  376.1 66.2 %collective-permute-start.17 = (bf16[512,1024]{1,0:T(8,128)(2,1)}, bf16[512,1024]{1,0:T(8,128)(2,1)}, u32[]{:S(2)}, u32[]{:S(2)}) collective-permute-start(bf16[512,1024]{1,0:T(8,128)(2,1)} %get-tuple-element.42), channel_id=1, source_target_pairs={{0,4},{4,0},{8,12},{12,8},{16,20},{20,16},{24,28},{28,24},{1,5},{5... | collective-permute-start | bytes 3145736 | tf_op jit(solution)/shard_map/ppermute | solution.py:173
  378.0 64.4 %collective-permute-start.16 = (bf16[512,1024]{1,0:T(8,128)(2,1)}, bf16[512,1024]{1,0:T(8,128)(2,1)}, u32[]{:S(2)}, u32[]{:S(2)}) collective-permute-start(bf16[512,1024]{1,0:T(8,128)(2,1)} %get-tuple-element.43), channel_id=1, source_target_pairs={{0,16},{4,20},{8,24},{12,28},{16,0},{20,4},{24,8},{28,12},{1,17},{... | collective-permute-start | bytes 3145736 | tf_op jit(solution)/shard_map/ppermute | solution.py:173
  (30 other events, 209.1 us)

commit v2 on v1

--- a/solution.py
+++ b/solution.py
@@ -132,80 +132,76 @@
     )(queries, keys, values, cosine, sine, probs, grads)
 
 
-def gather_cyclic(block):
-    n = lax.axis_size("tensor")
-    return [block] + [
-        lax.ppermute(block, "tensor", [(i, (i + s) % n) for i in range(n)]) for s in range(1, n)
-    ]
-
-
-def scatter_cyclic(term, rows):
-    n = lax.axis_size("tensor")
-    total = term[:rows].astype(F32)
-    for s in range(1, n):
-        part = term[s * rows : (s + 1) * rows]
-        total += lax.ppermute(part, "tensor", [(i, (i - s) % n) for i in range(n)]).astype(F32)
-    return total
-
-
-def scatter_groups(term):
+def after(value, *others):
+    return lax.optimization_barrier((value,) + others)[0]
+
+
+def gather_half(block):
+    return lax.all_gather(block, "tensor", axis=0, tiled=True)
+
+
+def scatter_half(term):
+    return lax.psum_scatter(term, "tensor", scatter_dimension=0, tiled=True)
+
+
+def group_blocks(term):
     n_dp, n_seq = lax.axis_size("dp"), lax.axis_size("seq")
-    dp, seq = lax.axis_index("dp"), lax.axis_index("seq")
+    return term.reshape(n_dp // 2, 2, n_seq * term.shape[0] // (n_dp * n_seq), term.shape[1])
+
+
+def core_exchange(term):
+    n_dp = lax.axis_size("dp")
+    core = lax.axis_index("dp") % 2
+    send = lax.dynamic_index_in_dim(group_blocks(term), 1 - core, 1, keepdims=False)
+    return lax.ppermute(send, "dp", [(i, i ^ 1) for i in range(n_dp)])
+
+
+def core_sum(term, came):
+    n_dp, n_seq = lax.axis_size("dp"), lax.axis_size("seq")
+    core = lax.axis_index("dp") % 2
+    keep = lax.dynamic_index_in_dim(group_blocks(term), core, 1, keepdims=False)
+    pair = (keep.astype(F32) + came.astype(F32)).astype(BF16)
     n = n_dp * n_seq
-    rows, columns = term.shape[0] // n, term.shape[1]
-    blocks = term.reshape(n_dp // 2, 2, n_seq * rows, columns)
-    core = dp % 2
-    send = lax.dynamic_index_in_dim(blocks, 1 - core, 1, keepdims=False)
-    keep = lax.dynamic_index_in_dim(blocks, core, 1, keepdims=False)
-    came = lax.ppermute(send, "dp", [(i, i ^ 1) for i in range(n_dp)])
-    pair = (keep.astype(F32) + came.astype(F32)).astype(BF16)
-    pair = pair.reshape(n // 2, rows, columns)
-    mine = (dp // 2) * n_seq + seq
-    total = lax.dynamic_index_in_dim(pair, mine, 0, keepdims=False).astype(F32)
+    return pair.reshape(n // 2, term.shape[0] // n, term.shape[1])
+
+
+def chip_exchange(pair):
+    n_dp, n_seq = lax.axis_size("dp"), lax.axis_size("seq")
+    n = n_dp * n_seq
+    mine = (lax.axis_index("dp") // 2) * n_seq + lax.axis_index("seq")
 
     def partner(i, d):
-        d_dp, d_seq = d // n_seq, d % n_seq
-        i_dp, i_seq = i // n_seq, i % n_seq
-        return (i_dp ^ (2 * d_dp)) * n_seq + (i_seq ^ d_seq)
-
+        return ((i // n_seq) ^ (2 * (d // n_seq))) * n_seq + ((i % n_seq) ^ (d % n_seq))
+
+    parts = [lax.dynamic_index_in_dim(pair, mine, 0, keepdims=False)]
     for d in range(n // 2 - 1, 0, -1):
         part = lax.dynamic_index_in_dim(pair, mine ^ d, 0, keepdims=False)
-        total += lax.ppermute(part, ("dp", "seq"), [(i, partner(i, d)) for i in range(n)]).astype(F32)
-    return total
+        parts.append(lax.ppermute(part, ("dp", "seq"), [(i, partner(i, d)) for i in range(n)]))
+    return parts
+
+
+def add_parts(parts):
+    return functools.reduce(lambda total, part: total + part.astype(F32), parts[1:], parts[0].astype(F32))
 
 
 def shards(
     lower, upper, grad_upper, grad_lower, positions, norm_gain, w_query, w_key, w_value, w_out
 ):
-    rows = lower.shape[0]
-    n_tensor = lax.axis_size("tensor")
+    half_rows = lower.shape[0] * lax.axis_size("tensor")
     n_seq = lax.axis_size("seq")
-    half_rows = rows * n_tensor
     k_width = w_key.shape[1]
-    me_t = lax.axis_index("tensor")
+    q_width = w_query.shape[1]
     me_s = lax.axis_index("seq")
 
-    lower_blocks = gather_cyclic(lower)
-    upstream_blocks = gather_cyclic(grad_upper)
-
-    local = jnp.concatenate(
-        [((me_t - s) % n_tensor) * rows + jnp.arange(rows, dtype=jnp.int32) for s in range(n_tensor)]
-    )
+    lower_rows = gather_half(lower)
+    upstream = gather_half(after(grad_upper, lower_rows))
+
+    local = jnp.arange(half_rows, dtype=jnp.int32)
     own_idx = me_s * half_rows + local
     key_idx = jnp.concatenate([((me_s + e) % n_seq) * half_rows + local for e in range(n_seq)])
-    own_pos = jnp.concatenate(
-        [
-            lax.dynamic_slice_in_dim(
-                positions[0], me_s * half_rows + ((me_t - s) % n_tensor) * rows, rows, 0
-            )
-            for s in range(n_tensor)
-        ]
-    )
+    own_pos = lax.dynamic_slice_in_dim(positions[0], me_s * half_rows, half_rows, 0)
     cosine, sine = tables(own_pos)
-
-    parts = [norm_rows(block, norm_gain) for block in lower_blocks]
-    normed_own, inverse_own, _ = parts[0]
-    hidden = jnp.concatenate([part[2] for part in parts], 0)
+    hidden = norm_rows(lower_rows, norm_gain)[2]
 
     def rope(values, sine_t):
         heads = values.reshape(half_rows, -1, HD)
@@ -225,12 +221,11 @@
         queries, keys_all, values_all, cosine, sine, own_idx, key_idx, own_pos
     )
     mixed_term = jnp.dot(attn, w_out, preferred_element_type=F32).astype(BF16)
-    mixed = scatter_cyclic(mixed_term, rows)
-    restored = (upper.astype(F32) - mixed).astype(BF16)
-
-    upstream = jnp.concatenate(upstream_blocks, 0)
+    upstream, mixed_term = lax.optimization_barrier((upstream, mixed_term))
+    mixed = scatter_half(mixed_term)
+
     out_term = contract_first(upstream, attn).astype(BF16)
-    grad_out = scatter_groups(out_term).T
+    out_came = core_exchange(out_term)
     grad_attn = contract_last(upstream, w_out).astype(BF16)
     dq, key_terms, value_terms = attention_backward(
         query_rot, keys_all, values_all, cosine, sine, probs, grad_attn
@@ -240,20 +235,30 @@
     for e in range(1, n_seq):
         part = terms[e * half_rows : (e + 1) * half_rows].astype(BF16)
         total += lax.ppermute(part, "seq", [(i, (i + e) % n_seq) for i in range(n_seq)]).astype(F32)
+    out_pair = core_sum(out_term, out_came)
+    out_pair, total = lax.optimization_barrier((out_pair, total))
+    out_parts = chip_exchange(out_pair)
     dk = rope(total[:, :k_width], -sine).astype(BF16)
     dv = total[:, k_width:].astype(BF16)
 
-    query_term = contract_first(hidden, dq).astype(BF16)
-    grad_query = scatter_groups(query_term)
-    kv_term = contract_first(hidden, jnp.concatenate([dk, dv], 1)).astype(BF16)
-    grad_kv = scatter_groups(kv_term)
-    grad_key, grad_value = grad_kv[:, :k_width], grad_kv[:, k_width:]
-
-    hidden_term = contract_last(dq, w_query) + contract_last(dk, w_key) + contract_last(dv, w_value)
-    grad_hidden = scatter_cyclic(hidden_term.astype(BF16), rows)
+    grads = jnp.concatenate([dq, dk, dv], 1)
+    weight_term = contract_first(hidden, after(grads, mixed, *out_parts[2:3])).astype(BF16)
+    weight_came = core_exchange(weight_term)
+    hidden_term = contract_last(after(dq, weight_term, *out_parts[1:]), w_query) + contract_last(dk, w_key) + contract_last(dv, w_value)
+    grad_hidden = scatter_half(hidden_term.astype(BF16)).astype(F32)
+    weight_pair = core_sum(weight_term, weight_came)
+    weight_pair, out_parts = lax.optimization_barrier((weight_pair, out_parts))
+    weight_parts = chip_exchange(weight_pair)
+
+    grad_out = add_parts(out_parts).T
+    restored = (upper.astype(F32) - mixed.astype(F32)).astype(BF16)
+    normed, inverse, _ = norm_rows(lower, norm_gain)
     scaled = norm_gain * grad_hidden
-    grad_in = inverse_own * (scaled - normed_own * jnp.mean(scaled * normed_own, -1, keepdims=True))
+    grad_in = inverse * (scaled - normed * jnp.mean(scaled * normed, -1, keepdims=True))
     grad_lower_in = (grad_lower.astype(F32) + grad_in).astype(BF16)
+    grad_query = add_parts([part[:, :q_width] for part in weight_parts])
+    grad_key = add_parts([part[:, q_width : q_width + k_width] for part in weight_parts])
+    grad_value = add_parts([part[:, q_width + k_width :] for part in weight_parts])
     return (restored, grad_lower_in, grad_query, grad_key, grad_value, grad_out)
 
 

time: 456 us -> 389 us (0.85); the launches traced: 447 us -> 388 us
  starting transfers between devices: 74.9 us -> 11.2 us
  waiting for transfers between devices: 224 us -> 206 us
  between operations: 1.86 us -> 14.2 us
  local copies, waits for them, and re-layouts: 40.1 us -> 45.9 us
  other arithmetic: 37.6 us -> 42.8 us
    ppermute x24 -> x8, waiting for transfers between devices: 224 us -> 89.9 us  [the longest x6 89.9 us: chip_exchange(): lax.ppermute(part, ('dp', 'seq'), [(i, partner(i, d)) for i in range(n)])]
    all_gather x0 -> x2, waiting for transfers between devices: none -> 76.6 us  [gather_half(): return lax.all_gather(block, 'tensor', axis=0, tiled=True)]
    ppermute x24 -> x8, starting transfers between devices: 72.7 us -> 7.89 us  [the longest x6 7.88 us: chip_exchange(): lax.ppermute(part, ('dp', 'seq'), [(i, partner(i, d)) for i in range(n)])]
    reduce_scatter x0 -> x2, waiting for transfers between devices: none -> 28.2 us  [scatter_half(): return lax.psum_scatter(term, 'tensor', scatter_dimension=0, tiled=True)]
    ppermute x1, waiting for transfers between devices: 0.01 us -> 8.65 us  [shards(): lax.ppermute(part, 'seq', [(i, (i + e) % n_seq) for i in range(n_seq)])]
    optimization_barrier x0 -> x1, local copies, waits for them, and re-layouts: none -> 6.22 us  [shards(): out_pair, total = lax.optimization_barrier((out_pair, total))]
    squeeze x6 -> x4, local copies, waits for them, and re-layouts: 11.3 us -> 16.3 us  [the longest x2 10.2 us: chip_exchange(): parts = [lax.dynamic_index_in_dim(pair, mine, 0, keepdims=False)]]
    convert_element_type x5 -> x4, other arithmetic: 17 us -> 20 us  [the longest x2 17.1 us: core_sum(): pair = (keep.astype(F32) + came.astype(F32)).astype(BF16)]
  transfers between devices with their start and end apart: 26 -> 14, of which waited for: 11 -> 9; matrix products, arithmetic and copies ran while one was open for 19% -> 25% of each run, Pallas kernels for 0% -> 4%
where the time goes in v2:
time: 389 us; the launch traced here: 388 us
  waiting for transfers between devices  206 us (53%)
  matrix products  51.4 us (13%)
  local copies, waits for them, and re-layouts  45.9 us (12%)
  other arithmetic  42.8 us (11%)
  Pallas kernels  16.7 us (4%)
  between operations  14.2 us (4%)
  starting transfers between devices  11.2 us (3%)
    ppermute x6, waiting for transfers between devices, chip_exchange(): lax.ppermute(part, ('dp', 'seq'), [(i, partner(i, d)) for i in range(n)])  89.9 us
    all_gather x2, waiting for transfers between devices, gather_half(): return lax.all_gather(block, 'tensor', axis=0, tiled=True)  76.6 us
    reduce_scatter x2, waiting for transfers between devices, scatter_half(): return lax.psum_scatter(term, 'tensor', scatter_dimension=0, tiled=True)  28.2 us
    dot_general x4, matrix products, contract_last(): lax.dot_general(left, right, (((1,), (1,)), ((), ())), preferred_element_...  22.4 us
    convert_element_type x2, other arithmetic, core_sum(): pair = (keep.astype(F32) + came.astype(F32)).astype(BF16)  17.1 us
    unnamed x55, local copies, waits for them, and re-layouts  16.8 us
    dot_general x2, matrix products, contract_first(): lax.dot_general(left, right, (((0,), (0,)), ((), ())), preferred_element_...  15.2 us
    squeeze x2, local copies, waits for them, and re-layouts, chip_exchange(): parts = [lax.dynamic_index_in_dim(pair, mine, 0, keepdims=False)]  10.2 us
  transfers between devices with their start and end apart: 14, of which 9 were waited for; matrix products, arithmetic and copies ran while one was open for 25% of the time, Pallas kernels for 4%

profile of v2, /device:TPU:0, one launch (start us, length us, event | category | flops | bytes accessed | tf_op | source)
XLA Modules:
  0.0 388.1 jit_solution(939230552031431372)
XLA Ops:
  11.3 55.8 %all-gather.3.cloned.1.call-done = bf16[320,4096]{1,0:T(8,128)(2,1)} async-done(((bf16[80,4096]{1,0:T(8,128)(2,1)}), bf16[320,4096]{1,0:T(8,128)(2,1)}) %all-gather.3.cloned.1.call-update) | async-done | bytes 2621456 | tf_op jit(solution)/shard_map/all_gather | solution.py:140
  67.2 2.5 fusion.4
  72.7 2.6 convolution_convert_fusion.4
  76.8 6.1 %fusion.23.q_ref = f32[320,1024]{1,0:T(8,128)S(1)} fusion(bf16[4096,1024]{1,0:T(8,128)(2,1)} %param.16, bf16[320,4096]{1,0:T(8,128)(2,1)S(1)} %copy-done.16, f32[4096]{0:T(1024)S(1)} %copy-done.24, f32[320]{0:T(512)S(1)} %add_rsqrt_fusion), kind=kOutput, calls=%fused_computation.76 | convolution fusion | flops 2689597440 | bytes 12338432 | tf_op jit(solution)/shard_map/dot_general | solution.py:219
  84.8 8.1 %attention_forward.1 = (bf16[320,1024]{1,0:T(8,128)(2,1)S(1)}, f32[8,320,640]{2,1,0:T(8,128)S(1)}, bf16[320,1024]{1,0:T(8,128)(2,1)S(1)}) custom-call(f32[320,1024]{1,0:T(8,128)S(1)} %fusion.23.q_ref, bf16[640,256]{1,0:T(8,128)(2,1)S(1)} %get-tuple-element.55.k_ref, bf16[640,256]{1,0:T(8,128)(2,1)S(1)} %get-tuple-element.54.v_ref, ...), custom_call_target="tpu_custom_call" | custom-call | flops 838860800 | bytes 6553600 | tf_op jit(solution)/shard_map/attention_forward/pallas_call | solution.py:96
  92.9 2.8 copy-done.1
  97.4 4.2 %convolution_convert_fusion.2 = bf16[320,4096]{1,0:T(8,128)(2,1)} fusion(bf16[320,1024]{1,0:T(8,128)(2,1)S(1)} %get-tuple-element.25, bf16[1024,4096]{1,0:T(8,128)(2,1)S(1)} %bitcast.78), kind=kOutput, calls=%fused_computation.12 | convolution fusion | flops 2685665280 | bytes 11665408 | tf_op jit(solution)/shard_map/dot_general | solution.py:223
  101.6 20.7 %all-gather.5.cloned.1.call-done = bf16[320,4096]{1,0:T(8,128)(2,1)} async-done(((bf16[80,4096]{1,0:T(8,128)(2,1)}), bf16[320,4096]{1,0:T(8,128)(2,1)}) %all-gather.5.cloned.1.call-update) | async-done | bytes 2621456 | tf_op jit(solution)/shard_map/all_gather | solution.py:140
  122.3 6.4 %convolution_convert_fusion.1 = bf16[4096,1024]{1,0:T(8,128)(2,1)S(1)} fusion(bf16[320,4096]{1,0:T(8,128)(2,1)} %all-gather.5.cloned.1.call-done, bf16[320,1024]{1,0:T(8,128)(2,1)} %copy-done.7), kind=kOutput, calls=%fused_computation.5 | convolution fusion | flops 2688548864 | bytes 11665408 | tf_op jit(solution)/shard_map/dot_general | solution.py:37
  128.8 2.8 dynamic-slice_bitcast_fusion.1
  133.8 7.1 %convolution_convert_fusion.3.g_ref = bf16[320,1024]{1,0:T(8,128)(2,1)S(1)} fusion(bf16[320,4096]{1,0:T(8,128)(2,1)} %all-gather.5.cloned.1.call-done, bf16[1024,4096]{1,0:T(8,128)(2,1)} %param.19), kind=kOutput, calls=%fused_computation.27 | convolution fusion | flops 2684682240 | bytes 11665408 | tf_op jit(solution)/shard_map/dot_general | solution.py:33
  140.9 2.9 copy-done.2
  143.8 8.5 %attention_backward.1 = (bf16[320,1024]{1,0:T(8,128)(2,1)S(1)}, f32[640,256]{1,0:T(8,128)S(1)}, f32[640,256]{1,0:T(8,128)S(1)}) custom-call(bf16[320,1024]{1,0:T(8,128)(2,1)S(1)} %copy-done.4, bf16[640,256]{1,0:T(8,128)(2,1)S(1)} %get-tuple-element.55.k_ref, bf16[640,256]{1,0:T(8,128)(2,1)S(1)} %get-tuple-element.54.v_ref, ...), custom_call_target="tpu_custom_call" | custom-call | flops 1677721600 | bytes 6553600 | tf_op jit(solution)/shard_map/attention_backward/pallas_call | solution.py:119
  155.7 8.6 %collective-permute-done.2 = bf16[320,512]{1,0:T(8,128)(2,1)S(1)} collective-permute-done((bf16[320,512]{1,0:T(8,128)(2,1)S(1)}, bf16[320,512]{1,0:T(8,128)(2,1)S(1)}, u32[]{:S(2)}, u32[]{:S(2)}) %collective-permute-start.2) | collective-permute-done | bytes 327712 | tf_op jit(solution)/shard_map/ppermute | solution.py:237
  165.6 7.7 %fusion.1 = bf16[2,1024,1024]{2,1,0:T(8,128)(2,1)} fusion(bf16[2,1024,1024]{2,1,0:T(8,128)(2,1)} %collective-permute-done.1, bf16[2,2,1024,1024]{3,2,1,0:T(8,128)(2,1)} %bitcast.72, s32[]{:T(128)S(6)} %select_n.61), kind=kLoop, calls=%fused_computation.4 | loop fusion | flops 8388608 | bytes 12582916 | tf_op jit(solution)/shard_map/convert_element_type | solution.py:163
  173.3 6.2 %copy.21 = bf16[4,512,1024]{1,2,0:T(8,128)(2,1)} copy(bf16[4,512,1024]{2,1,0:T(8,128)(2,1)} %bitcast.68) | data formatting | bytes 8388608 | tf_op jit(solution)/shard_map/optimization_barrier | solution.py:239
  179.5 4.3 %dynamic-slice_bitcast_fusion.6 = (bf16[512,1024]{0,1:T(8,128)(2,1)}, bf16[512,1024]{0,1:T(8,128)(2,1)}, bf16[512,1024]{0,1:T(8,128)(2,1)}, bf16[512,1024]{0,1:T(8,128)(2,1)}) fusion(bf16[4,512,1024]{1,2,0:T(8,128)(2,1)} %copy.21, s32[]{:T(128)S(6)} %select_n.67, s32[]{:T(128)S(6)} %select_n.66, s32[]{:T(128)S(6)} %select_n.65, s32[]{:T(128)S(6)} %select_n.64), kind=kLoop, calls=%fused_computation.37 | loop fusion | bytes 8388624 | tf_op jit(solution)/shard_map/jit(dynamic_index_in_dim)/squeeze | solution.py:176
  193.3 15.7 %collective-permute-done.3 = bf16[512,1024]{0,1:T(8,128)(2,1)} collective-permute-done((bf16[512,1024]{0,1:T(8,128)(2,1)}, bf16[512,1024]{0,1:T(8,128)(2,1)}, u32[]{:S(2)}, u32[]{:S(2)}) %collective-permute-start.3) | collective-permute-done | bytes 1048608 | tf_op jit(solution)/shard_map/ppermute | solution.py:179
  209.0 8.8 %convolution_convert_fusion = bf16[4096,1536]{1,0:T(8,128)(2,1)S(1)} fusion(bf16[320,1536]{1,0:T(8,128)(2,1)} %pad_maximum_fusion, bf16[320,4096]{1,0:T(8,128)(2,1)} %all-gather.3.cloned.1.call-done, f32[4096]{0:T(1024)S(1)} %copy-done.24, f32[320]{0:T(512)S(1)} %add_rsqrt_fusion), kind=kOutput, calls=%fused_computation | convolution fusion | flops 4038066176 | bytes 16205056 | tf_op jit(solution)/shard_map/dot_general | solution.py:37
  217.8 3.3 dynamic-slice_bitcast_fusion
  221.2 3.2 copy-done.8
  228.3 3.3 fusion.29
  231.6 19.6 %collective-permute-done.4 = bf16[512,1024]{0,1:T(8,128)(2,1)} collective-permute-done((bf16[512,1024]{0,1:T(8,128)(2,1)}, bf16[512,1024]{0,1:T(8,128)(2,1)}, u32[]{:S(2)}, u32[]{:S(2)}) %collective-permute-start.4) | collective-permute-done | bytes 1048608 | tf_op jit(solution)/shard_map/ppermute | solution.py:179
  251.2 22.4 %collective-permute-done.5 = bf16[512,1024]{0,1:T(8,128)(2,1)} collective-permute-done((bf16[512,1024]{0,1:T(8,128)(2,1)}, bf16[512,1024]{0,1:T(8,128)(2,1)}, u32[]{:S(2)}, u32[]{:S(2)}) %collective-permute-start.5) | collective-permute-done | bytes 1048608 | tf_op jit(solution)/shard_map/ppermute | solution.py:179
  273.6 11.1 %fusion.3 = bf16[320,4096]{1,0:T(8,128)(2,1)} fusion(f32[320,4096]{1,0:T(8,128)} %fusion.29, f32[320,4096]{1,0:T(8,128)S(1)} %fusion.31, bf16[320,1024]{1,0:T(8,128)(2,1)S(1)} %copy-done.6, bf16[4096,1024]{1,0:T(8,128)(2,1)} %param.16), kind=kOutput, calls=%fused_computation.11 | convolution fusion | flops 2688286720 | bytes 22151168 | tf_op jit(solution)/shard_map/dot_general | solution.py:33
  288.1 9.4 %fusion = bf16[2,1024,1536]{2,1,0:T(8,128)(2,1)} fusion(bf16[2,1024,1536]{2,1,0:T(8,128)(2,1)} %collective-permute-done.6, bf16[2,2,1024,1536]{3,2,1,0:T(8,128)(2,1)} %bitcast.70, s32[]{:T(128)S(6)} %select_n.61), kind=kLoop, calls=%fused_computation.2 | loop fusion | flops 12582912 | bytes 18874372 | tf_op jit(solution)/shard_map/convert_element_type | solution.py:163
  297.5 5.8 %dynamic-slice_bitcast_fusion.5 = (bf16[512,1536]{1,0:T(8,128)(2,1)}, bf16[512,1536]{1,0:T(8,128)(2,1)}, bf16[512,1536]{1,0:T(8,128)(2,1)}, bf16[512,1536]{1,0:T(8,128)(2,1)}) fusion(bf16[4,512,1536]{2,1,0:T(8,128)(2,1)} %bitcast.67, s32[]{:T(128)S(6)} %select_n.67, s32[]{:T(128)S(6)} %select_n.66, s32[]{:T(128)S(6)} %select_n.64, s32[]{:T(128)S(6)} %select_n.65), kind=kLoop, calls=%fused_computation.24 | loop fusion | bytes 12582928 | tf_op jit(solution)/shard_map/jit(dynamic_index_in_dim)/squeeze | solution.py:176
  306.9 28.2 %reduce-scatter.5.cloned.1.call-done = bf16[80,4096]{1,0:T(8,128)(2,1)} async-done(((bf16[320,4096]{1,0:T(8,128)(2,1)}), bf16[80,4096]{1,0:T(8,128)(2,1)}) %reduce-scatter.5.cloned.1.call-update) | async-done | bytes 655376 | tf_op jit(solution)/shard_map/reduce_scatter | solution.py:144
  339.0 3.8 add_bitcast_fusion
  342.9 32.2 %collective-permute-done.7 = bf16[512,1536]{1,0:T(8,128)(2,1)} collective-permute-done((bf16[512,1536]{1,0:T(8,128)(2,1)}, bf16[512,1536]{1,0:T(8,128)(2,1)}, u32[]{:S(2)}, u32[]{:S(2)}) %collective-permute-start.7) | collective-permute-done | bytes 1572896 | tf_op jit(solution)/shard_map/ppermute | solution.py:179
  375.0 3.9 %convert_add_fusion.2 = f32[512,1024]{1,0:T(8,128)} fusion(bf16[512,1536]{1,0:T(8,128)(2,1)} %collective-permute-done.9, bf16[512,1536]{1,0:T(8,128)(2,1)} %collective-permute-done.8, bf16[512,1536]{1,0:T(8,128)(2,1)} %collective-permute-done.7, bf16[512,1536]{1,0:T(8,128)(2,1)S(1)} %copy-done.11), kind=kLoop, calls=%fused_computation.18 | loop fusion | flops 3670016 | bytes 6291456 | tf_op jit(solution)/shard_map/add | solution.py:184
  378.9 2.6 convert_add_fusion.3
  (114 shorter events, 43.0 us)
Async XLA Ops:
  7.2 62.6 %copy-start = (bf16[4096,256]{1,0:T(8,128)(2,1)S(1)}, bf16[4096,256]{1,0:T(8,128)(2,1)}, u32[]{:S(2)}) copy-start(bf16[4096,256]{1,0:T(8,128)(2,1)} %param.17) | copy-start | bytes 6291460
  7.2 59.9 %all-gather.3.cloned.1.call-start = ((), (), s32[]{:S(2)}) async-start(), calls=%async_computation.2 | async-start | bytes 3276800 | tf_op jit(solution)/shard_map/all_gather | solution.py:140
  7.9 61.8 %copy-start.24 = (f32[4096]{0:T(1024)S(1)}, f32[4096]{0:T(1024)}, u32[]{:S(2)}) copy-start(f32[4096]{0:T(1024)} %param.15) | copy-start | bytes 49156
  7.9 114.4 %all-gather.5.cloned.1.call-start = ((), (), s32[]{:S(2)}) async-start(), calls=%async_computation.3 | async-start | bytes 3276800 | tf_op jit(solution)/shard_map/all_gather | solution.py:140
  67.2 126.1 %reduce-scatter.3.cloned.1.call-start = ((), (), s32[]{:S(2)}) async-start(), calls=%async_computation.4 | async-start | bytes 3276800 | tf_op jit(solution)/shard_map/reduce_scatter | solution.py:144
  67.2 2.5 copy-start.15
  70.9 1.8 copy-start.16
  75.3 22.1 %slice-start = ((s8[8388608]{0:T(1024)(128)(4,1)}), s8[4194304]{0:T(1024)(128)(4,1)S(1)}, s32[]{:S(2)}) async-start(s8[8388608]{0:T(1024)(128)(4,1)} %bitcast.77), calls=%async_computation.6 | async-start | bytes 8388608
  75.3 22.1 %slice-start.1 = ((s8[8388608]{0:T(1024)(128)(4,1)}), s8[4194304]{0:T(1024)(128)(4,1)S(1)}, s32[]{:S(2)}) async-start(s8[8388608]{0:T(1024)(128)(4,1)} %bitcast.77), calls=%async_computation.7 | async-start | bytes 8388608
  75.3 9.4 %collective-permute-start = (bf16[320,512]{1,0:T(8,128)(2,1)S(1)}, bf16[320,512]{1,0:T(8,128)(2,1)S(1)}, u32[]{:S(2)}, u32[]{:S(2)}) collective-permute-start(bf16[320,512]{1,0:T(8,128)(2,1)S(1)} %pad_maximum_fusion.2), channel_id=1, source_target_pairs={{0,4},{4,0},{1,5},{5,1},{2,6},{6,2},{3,7},{7,3},{8,12},{12,8},{9,1... | collective-permute-start | bytes 983048 | tf_op jit(solution)/shard_map/ppermute | solution.py:216
  92.9 2.8 copy-start.1
  128.8 4.8 %copy-start.10 = (bf16[4096,1024]{1,0:T(8,128)(2,1)}, bf16[4096,1024]{1,0:T(8,128)(2,1)S(1)}, u32[]{:S(2)}) copy-start(bf16[4096,1024]{1,0:T(8,128)(2,1)S(1)} %convolution_convert_fusion.1) | copy-start | bytes 25165828
  133.5 32.0 %collective-permute-start.1 = (bf16[2,1024,1024]{2,1,0:T(8,128)(2,1)}, bf16[2,1024,1024]{2,1,0:T(8,128)(2,1)}, u32[]{:S(2)}, u32[]{:S(2)}) collective-permute-start(bf16[2,1024,1024]{2,1,0:T(8,128)(2,1)} %dynamic-slice_bitcast_fusion.1), channel_id=1, source_target_pairs={{0,8},{8,0},{16,24},{24,16},{1,9},{9,1},{17,25},{25,17},{2,10},{10... | collective-permute-start | bytes 12582920 | tf_op jit(solution)/shard_map/ppermute | solution.py:156
  133.5 201.5 %reduce-scatter.5.cloned.1.call-start = ((), (), s32[]{:S(2)}) async-start(), calls=%async_computation.5 | async-start | bytes 3276800 | tf_op jit(solution)/shard_map/reduce_scatter | solution.py:144
  133.8 7.2 %copy-start.4 = (bf16[320,1024]{1,0:T(8,128)(2,1)S(1)}, bf16[320,1024]{1,0:T(8,128)(2,1)}, u32[]{:S(2)}) copy-start(bf16[320,1024]{1,0:T(8,128)(2,1)} %copy-done.3) | copy-start | bytes 1966084
  140.9 2.9 copy-start.2
  154.2 10.1 %collective-permute-start.2 = (bf16[320,512]{1,0:T(8,128)(2,1)S(1)}, bf16[320,512]{1,0:T(8,128)(2,1)S(1)}, u32[]{:S(2)}, u32[]{:S(2)}) collective-permute-start(bf16[320,512]{1,0:T(8,128)(2,1)S(1)} %slice.127), channel_id=1, source_target_pairs={{0,4},{4,0},{1,5},{5,1},{2,6},{6,2},{3,7},{7,3},{8,12},{12,8},{9,1... | collective-permute-start | bytes 983048 | tf_op jit(solution)/shard_map/ppermute | solution.py:237
  183.8 8.4 %copy-start.6 = (bf16[320,1024]{1,0:T(8,128)(2,1)S(1)}, bf16[320,1024]{1,0:T(8,128)(2,1)}, u32[]{:S(2)}) copy-start(bf16[320,1024]{1,0:T(8,128)(2,1)} %copy-done.5) | copy-start | bytes 1966084
  183.8 25.2 %collective-permute-start.3 = (bf16[512,1024]{0,1:T(8,128)(2,1)}, bf16[512,1024]{0,1:T(8,128)(2,1)}, u32[]{:S(2)}, u32[]{:S(2)}) collective-permute-start(bf16[512,1024]{0,1:T(8,128)(2,1)} %get-tuple-element.53), channel_id=1, source_target_pairs={{0,16},{4,20},{8,24},{12,28},{16,0},{20,4},{24,8},{28,12},{1,17},{... | collective-permute-start | bytes 3145736 | tf_op jit(solution)/shard_map/ppermute | solution.py:179
  188.6 2.9 copy-start.14
  188.6 3.7 copy-start.23
  217.8 6.5 %copy-start.8 = (bf16[4096,1536]{1,0:T(8,128)(2,1)}, bf16[4096,1536]{1,0:T(8,128)(2,1)S(1)}, u32[]{:S(2)}) copy-start(bf16[4096,1536]{1,0:T(8,128)(2,1)S(1)} %convolution_convert_fusion) | copy-start | bytes 37748740
  217.8 9.4 %copy-start.18 = (bf16[320,256]{1,0:T(8,128)(2,1)S(1)}, bf16[320,256]{1,0:T(8,128)(2,1)}, u32[]{:S(2)}) copy-start(bf16[320,256]{1,0:T(8,128)(2,1)} %copy-done.17) | copy-start | bytes 491524
  224.3 63.8 %collective-permute-start.6 = (bf16[2,1024,1536]{2,1,0:T(8,128)(2,1)}, bf16[2,1024,1536]{2,1,0:T(8,128)(2,1)}, u32[]{:S(2)}, u32[]{:S(2)}) collective-permute-start(bf16[2,1024,1536]{2,1,0:T(8,128)(2,1)} %dynamic-slice_bitcast_fusion), channel_id=1, source_target_pairs={{0,8},{8,0},{16,24},{24,16},{1,9},{9,1},{17,25},{25,17},{2,10},{10... | collective-permute-start | bytes 18874376 | tf_op jit(solution)/shard_map/ppermute | solution.py:156
  224.3 26.9 %collective-permute-start.4 = (bf16[512,1024]{0,1:T(8,128)(2,1)}, bf16[512,1024]{0,1:T(8,128)(2,1)}, u32[]{:S(2)}, u32[]{:S(2)}) collective-permute-start(bf16[512,1024]{0,1:T(8,128)(2,1)} %get-tuple-element.52), channel_id=1, source_target_pairs={{0,20},{4,16},{8,28},{12,24},{16,4},{20,0},{24,12},{28,8},{1,21},{... | collective-permute-start | bytes 3145736 | tf_op jit(solution)/shard_map/ppermute | solution.py:179
  226.7 46.9 %collective-permute-start.5 = (bf16[512,1024]{0,1:T(8,128)(2,1)}, bf16[512,1024]{0,1:T(8,128)(2,1)}, u32[]{:S(2)}, u32[]{:S(2)}) collective-permute-start(bf16[512,1024]{0,1:T(8,128)(2,1)} %get-tuple-element.51), channel_id=1, source_target_pairs={{0,4},{4,0},{8,12},{12,8},{16,20},{20,16},{24,28},{28,24},{1,5},{5... | collective-permute-start | bytes 3145736 | tf_op jit(solution)/shard_map/ppermute | solution.py:179
  297.5 39.1 %copy-start.22 = (bf16[80,4096]{1,0:T(8,128)(2,1)S(1)}, bf16[80,4096]{1,0:T(8,128)(2,1)}, u32[]{:S(2)}) copy-start(bf16[80,4096]{1,0:T(8,128)(2,1)} %param.13) | copy-start | bytes 1966084
  303.4 39.5 %collective-permute-start.9 = (bf16[512,1536]{1,0:T(8,128)(2,1)}, bf16[512,1536]{1,0:T(8,128)(2,1)}, u32[]{:S(2)}, u32[]{:S(2)}) collective-permute-start(bf16[512,1536]{1,0:T(8,128)(2,1)} %get-tuple-element.47), channel_id=1, source_target_pairs={{0,4},{4,0},{8,12},{12,8},{16,20},{20,16},{24,28},{28,24},{1,5},{5... | collective-permute-start | bytes 4718600 | tf_op jit(solution)/shard_map/ppermute | solution.py:179
  305.0 37.9 %collective-permute-start.8 = (bf16[512,1536]{1,0:T(8,128)(2,1)}, bf16[512,1536]{1,0:T(8,128)(2,1)}, u32[]{:S(2)}, u32[]{:S(2)}) collective-permute-start(bf16[512,1536]{1,0:T(8,128)(2,1)} %get-tuple-element.48), channel_id=1, source_target_pairs={{0,16},{4,20},{8,24},{12,28},{16,0},{20,4},{24,8},{28,12},{1,17},{... | collective-permute-start | bytes 4718600 | tf_op jit(solution)/shard_map/ppermute | solution.py:179
  305.7 69.3 %collective-permute-start.7 = (bf16[512,1536]{1,0:T(8,128)(2,1)}, bf16[512,1536]{1,0:T(8,128)(2,1)}, u32[]{:S(2)}, u32[]{:S(2)}) collective-permute-start(bf16[512,1536]{1,0:T(8,128)(2,1)} %get-tuple-element.49), channel_id=1, source_target_pairs={{0,20},{4,16},{8,28},{12,24},{16,4},{20,0},{24,12},{28,8},{1,21},{... | collective-permute-start | bytes 4718600 | tf_op jit(solution)/shard_map/ppermute | solution.py:179
  335.0 4.0 %copy-start.12 = (bf16[512,1024]{0,1:T(8,128)(2,1)S(1)}, bf16[512,1024]{0,1:T(8,128)(2,1)}, u32[]{:S(2)}) copy-start(bf16[512,1024]{0,1:T(8,128)(2,1)} %get-tuple-element.38) | copy-start | bytes 3145732
  339.0 36.0 %copy-start.11 = (bf16[512,1536]{1,0:T(8,128)(2,1)S(1)}, bf16[512,1536]{1,0:T(8,128)(2,1)}, u32[]{:S(2)}) copy-start(bf16[512,1536]{1,0:T(8,128)(2,1)} %get-tuple-element.46) | copy-start | bytes 4718596
  (9 other events, 9.0 us)
Sparse Core Ops, SparseCore 0:
  9.6 57.4 all-gather.2
  68.7 53.5 all-gather.4
  133.7 51.0 reduce-scatter.2
  284.9 50.1 reduce-scatter.4

commit v3 on v2

--- a/solution.py
+++ b/solution.py
@@ -156,28 +156,75 @@
     return lax.ppermute(send, "dp", [(i, i ^ 1) for i in range(n_dp)])
 
 
+def chip_partner(i, d):
+    n_seq = lax.axis_size("seq")
+    return ((i // n_seq) ^ (2 * (d // n_seq))) * n_seq + ((i % n_seq) ^ (d % n_seq))
+
+
+def pair_body(count, index_ref, *refs):
+    for d in range(count):
+        total = refs[d][...].astype(F32) + refs[count + d][...].astype(F32)
+        refs[2 * count + d][...] = total[0].astype(BF16)
+
+
 def core_sum(term, came):
     n_dp, n_seq = lax.axis_size("dp"), lax.axis_size("seq")
-    core = lax.axis_index("dp") % 2
-    keep = lax.dynamic_index_in_dim(group_blocks(term), core, 1, keepdims=False)
-    pair = (keep.astype(F32) + came.astype(F32)).astype(BF16)
     n = n_dp * n_seq
-    return pair.reshape(n // 2, term.shape[0] // n, term.shape[1])
+    count, rows, columns = n // 2, term.shape[0] // n, term.shape[1]
+    dp, seq = lax.axis_index("dp"), lax.axis_index("seq")
+    me, mine = dp * n_seq + seq, (dp // 2) * n_seq + seq
+    index = jnp.stack(
+        [chip_partner(me, d) for d in range(count)] + [mine ^ d for d in range(count)]
+    ).astype(jnp.int32)
+    tile = math.gcd(128, rows)
+
+    def at(place):
+        return pl.BlockSpec((1, tile, columns), lambda t, index_ref: (index_ref[place], t, 0))
+
+    return pl.pallas_call(
+        functools.partial(pair_body, count),
+        grid_spec=pltpu.PrefetchScalarGridSpec(
+            num_scalar_prefetch=1,
+            grid=(rows // tile,),
+            in_specs=[at(place) for place in range(2 * count)],
+            out_specs=[pl.BlockSpec((tile, columns), lambda t, index_ref: (t, 0))] * count,
+        ),
+        out_shape=[jax.ShapeDtypeStruct((rows, columns), BF16)] * count,
+        compiler_params=pltpu.CompilerParams(vmem_limit_bytes=VMEM_LIMIT),
+        cost_estimate=pl.CostEstimate(
+            flops=count * rows * columns, bytes_accessed=6 * count * rows * columns, transcendentals=0
+        ),
+        name="core_sum",
+    )(index, *[term.reshape(n, rows, columns)] * count, *[came.reshape(count, rows, columns)] * count)
 
 
 def chip_exchange(pair):
-    n_dp, n_seq = lax.axis_size("dp"), lax.axis_size("seq")
-    n = n_dp * n_seq
-    mine = (lax.axis_index("dp") // 2) * n_seq + lax.axis_index("seq")
-
-    def partner(i, d):
-        return ((i // n_seq) ^ (2 * (d // n_seq))) * n_seq + ((i % n_seq) ^ (d % n_seq))
-
-    parts = [lax.dynamic_index_in_dim(pair, mine, 0, keepdims=False)]
+    n = lax.axis_size("dp") * lax.axis_size("seq")
+    parts = [pair[0]]
     for d in range(n // 2 - 1, 0, -1):
-        part = lax.dynamic_index_in_dim(pair, mine ^ d, 0, keepdims=False)
-        parts.append(lax.ppermute(part, ("dp", "seq"), [(i, partner(i, d)) for i in range(n)]))
+        ways = [(i, chip_partner(i, d)) for i in range(n)]
+        parts.append(lax.ppermute(pair[d], ("dp", "seq"), ways))
     return parts
+
+
+def turned_body(*refs):
+    total = refs[0][...].astype(F32)
+    for ref in refs[1:-1]:
+        total += ref[...].astype(F32)
+    refs[-1][...] = total.T
+
+
+def add_turned(parts):
+    rows, columns = parts[0].shape
+    return pl.pallas_call(
+        turned_body,
+        grid=(columns // HD,),
+        in_specs=[pl.BlockSpec((rows, HD), lambda c: (0, c))] * len(parts),
+        out_specs=pl.BlockSpec((HD, rows), lambda c: (c, 0)),
+        out_shape=jax.ShapeDtypeStruct((columns, rows), F32),
+        compiler_params=pltpu.CompilerParams(vmem_limit_bytes=VMEM_LIMIT),
+        name="add_turned",
+    )(*parts)
 
 
 def add_parts(parts):
@@ -232,25 +279,34 @@
     )
     terms = jnp.concatenate([key_terms, value_terms], 1)
     total = terms[:half_rows]
-    for e in range(1, n_seq):
-        part = terms[e * half_rows : (e + 1) * half_rows].astype(BF16)
-        total += lax.ppermute(part, "seq", [(i, (i + e) % n_seq) for i in range(n_seq)]).astype(F32)
+    came = [
+        lax.ppermute(
+            terms[e * half_rows : (e + 1) * half_rows].astype(BF16),
+            "seq",
+            [(i, (i + e) % n_seq) for i in range(n_seq)],
+        )
+        for e in range(1, n_seq)
+    ]
     out_pair = core_sum(out_term, out_came)
-    out_pair, total = lax.optimization_barrier((out_pair, total))
+    came, out_pair = lax.optimization_barrier((came, out_pair))
     out_parts = chip_exchange(out_pair)
+    total = add_parts([total] + came)
     dk = rope(total[:, :k_width], -sine).astype(BF16)
     dv = total[:, k_width:].astype(BF16)
 
     grads = jnp.concatenate([dq, dk, dv], 1)
-    weight_term = contract_first(hidden, after(grads, mixed, *out_parts[2:3])).astype(BF16)
+    weight_term = contract_first(hidden, after(grads, mixed, *out_parts[2:])).astype(BF16)
+    dq, dk, dv, weight_term = lax.optimization_barrier((dq, dk, dv, weight_term))
     weight_came = core_exchange(weight_term)
-    hidden_term = contract_last(after(dq, weight_term, *out_parts[1:]), w_query) + contract_last(dk, w_key) + contract_last(dv, w_value)
-    grad_hidden = scatter_half(hidden_term.astype(BF16)).astype(F32)
+    hidden_term = contract_last(dq, w_query) + contract_last(after(dk, out_parts[1]), w_key) + contract_last(dv, w_value)
+    hidden_term = hidden_term.astype(BF16)
+    grad_hidden = scatter_half(hidden_term).astype(F32)
+    weight_came = after(weight_came, hidden_term)
     weight_pair = core_sum(weight_term, weight_came)
     weight_pair, out_parts = lax.optimization_barrier((weight_pair, out_parts))
     weight_parts = chip_exchange(weight_pair)
 
-    grad_out = add_parts(out_parts).T
+    grad_out = add_turned(out_parts)
     restored = (upper.astype(F32) - mixed.astype(F32)).astype(BF16)
     normed, inverse, _ = norm_rows(lower, norm_gain)
     scaled = norm_gain * grad_hidden

time: 389 us -> 334 us (0.86)
  waiting for transfers between devices: 206 us -> 176 us
  Pallas kernels: 16.7 us -> 37.6 us
  other arithmetic: 42.8 us -> 22.1 us
  local copies, waits for them, and re-layouts: 45.9 us -> 28.8 us
  matrix products: 51.4 us -> 44.8 us
    ppermute x7, waiting for transfers between devices: 98.5 us -> 51.6 us  [the longest x6 49.8 us: chip_exchange(): parts.append(lax.ppermute(pair[d], ('dp', 'seq'), ways))]
    pallas_call x0 -> x3, Pallas kernels: none -> 20.9 us  [the longest x2 14.3 us: core_sum(): pl.pallas_call(functools.partial(pair_body, count), grid_spec=pltpu.Prefe...]
    convert_element_type x2 -> x0, other arithmetic: 17.1 us -> none  [core_sum(): pair = (keep.astype(F32) + came.astype(F32)).astype(BF16)]
    reduce_scatter x2, waiting for transfers between devices: 28.2 us -> 44.9 us  [scatter_half(): return lax.psum_scatter(term, 'tensor', scatter_dimension=0, tiled=True)]
    squeeze x2 -> x0, local copies, waits for them, and re-layouts: 10.2 us -> none  [chip_exchange(): parts = [lax.dynamic_index_in_dim(pair, mine, 0, keepdims=False)]]
    dot_general x4, matrix products: 22.4 us -> 15.8 us  [contract_last(): lax.dot_general(left, right, (((1,), (1,)), ((), ())), preferred_element_...]
    optimization_barrier x1 -> x0, local copies, waits for them, and re-layouts: 6.22 us -> none  [shards(): out_pair, total = lax.optimization_barrier((out_pair, total))]
    unnamed x55 -> x61, local copies, waits for them, and re-layouts: 16.8 us -> 18 us
  transfers between devices with their start and end apart: 14 -> 14, of which waited for: 9 -> 10; matrix products, arithmetic and copies ran while one was open for 25% -> 19% of each run, Pallas kernels for 4% -> 11%
where the time goes in v3:
time: 334 us
  waiting for transfers between devices  176 us (53%)
  matrix products  44.8 us (13%)
  Pallas kernels  37.6 us (11%)
  local copies, waits for them, and re-layouts  28.8 us (9%)
  other arithmetic  22.1 us (7%)
  between operations  14.3 us (4%)
  starting transfers between devices  10.3 us (3%)
    all_gather x2, waiting for transfers between devices, gather_half(): return lax.all_gather(block, 'tensor', axis=0, tiled=True)  76.6 us
    ppermute x6, waiting for transfers between devices, chip_exchange(): parts.append(lax.ppermute(pair[d], ('dp', 'seq'), ways))  49.8 us
    reduce_scatter x2, waiting for transfers between devices, scatter_half(): return lax.psum_scatter(term, 'tensor', scatter_dimension=0, tiled=True)  44.9 us
    unnamed x61, local copies, waits for them, and re-layouts  18 us
    dot_general x4, matrix products, contract_last(): lax.dot_general(left, right, (((1,), (1,)), ((), ())), preferred_element_...  15.8 us
    dot_general x2, matrix products, contract_first(): lax.dot_general(left, right, (((0,), (0,)), ((), ())), preferred_element_...  15.2 us
    pallas_call x2, Pallas kernels, core_sum(): pl.pallas_call(functools.partial(pair_body, count), grid_spec=pltpu.Prefe...  14.3 us
    pallas_call x1, Pallas kernels, attention_backward(): pl.pallas_call(functools.partial(backward_body, group), grid=(heads,), in...  8.55 us
  transfers between devices with their start and end apart: 14, of which 10 were waited for; matrix products, arithmetic and copies ran while one was open for 19% of the time, Pallas kernels for 11%

profile of v3, /device:TPU:0, one launch (start us, length us, event | category | flops | bytes accessed | tf_op | source)
XLA Modules:
  0.0 333.6 jit_solution(8863120158202647166)
XLA Ops:
  11.3 55.9 %all-gather.3.cloned.1.call-done = bf16[320,4096]{1,0:T(8,128)(2,1)} async-done(((bf16[80,4096]{1,0:T(8,128)(2,1)}), bf16[320,4096]{1,0:T(8,128)(2,1)}) %all-gather.3.cloned.1.call-update) | async-done | bytes 2621456 | tf_op jit(solution)/shard_map/all_gather | solution.py:140
  67.2 2.5 fusion.1
  72.7 2.6 convolution_convert_fusion.4
  76.8 6.1 %fusion.20.q_ref = f32[320,1024]{1,0:T(8,128)S(1)} fusion(bf16[4096,1024]{1,0:T(8,128)(2,1)} %param.16, bf16[320,4096]{1,0:T(8,128)(2,1)S(1)} %copy-done.19, f32[4096]{0:T(1024)S(1)} %copy-done.27, f32[320]{0:T(512)S(1)} %add_rsqrt_fusion), kind=kOutput, calls=%fused_computation.63 | convolution fusion | flops 2689597440 | bytes 12338432 | tf_op jit(solution)/shard_map/dot_general | solution.py:266
  82.9 1.8 collective-permute-done
  84.8 8.1 %attention_forward.1 = (bf16[320,1024]{1,0:T(8,128)(2,1)S(1)}, f32[8,320,640]{2,1,0:T(8,128)S(1)}, bf16[320,1024]{1,0:T(8,128)(2,1)S(1)}) custom-call(f32[320,1024]{1,0:T(8,128)S(1)} %fusion.20.q_ref, bf16[640,256]{1,0:T(8,128)(2,1)S(1)} %get-tuple-element.85.k_ref, bf16[640,256]{1,0:T(8,128)(2,1)S(1)} %get-tuple-element.84.v_ref, ...), custom_call_target="tpu_custom_call" | custom-call | flops 838860800 | bytes 6553600 | tf_op jit(solution)/shard_map/attention_forward/pallas_call | solution.py:96
  92.9 2.8 copy-done.1
  97.4 4.2 %convolution_convert_fusion.2 = bf16[320,4096]{1,0:T(8,128)(2,1)} fusion(bf16[320,1024]{1,0:T(8,128)(2,1)S(1)} %get-tuple-element.44, bf16[1024,4096]{1,0:T(8,128)(2,1)S(1)} %bitcast.69), kind=kOutput, calls=%fused_computation.8 | convolution fusion | flops 2685665280 | bytes 11665408 | tf_op jit(solution)/shard_map/dot_general | solution.py:270
  101.5 20.8 %all-gather.5.cloned.1.call-done = bf16[320,4096]{1,0:T(8,128)(2,1)} async-done(((bf16[80,4096]{1,0:T(8,128)(2,1)}), bf16[320,4096]{1,0:T(8,128)(2,1)}) %all-gather.5.cloned.1.call-update) | async-done | bytes 2621456 | tf_op jit(solution)/shard_map/all_gather | solution.py:140
  122.3 6.4 %convolution_convert_fusion.1 = bf16[4096,1024]{1,0:T(8,128)(2,1)S(1)} fusion(bf16[320,4096]{1,0:T(8,128)(2,1)} %all-gather.5.cloned.1.call-done, bf16[320,1024]{1,0:T(8,128)(2,1)} %copy-done.11), kind=kOutput, calls=%fused_computation.1 | convolution fusion | flops 2688548864 | bytes 11665408 | tf_op jit(solution)/shard_map/dot_general | solution.py:37
  128.8 2.8 dynamic-slice_bitcast_fusion.1
  131.6 1.9 copy-done.13
  133.8 7.1 %convolution_convert_fusion.3.g_ref = bf16[320,1024]{1,0:T(8,128)(2,1)S(1)} fusion(bf16[320,4096]{1,0:T(8,128)(2,1)} %all-gather.5.cloned.1.call-done, bf16[1024,4096]{1,0:T(8,128)(2,1)} %param.19), kind=kOutput, calls=%fused_computation.18 | convolution fusion | flops 2684682240 | bytes 11665408 | tf_op jit(solution)/shard_map/dot_general | solution.py:33
  140.9 2.9 copy-done.2
  143.8 8.6 %attention_backward.1 = (bf16[320,1024]{1,0:T(8,128)(2,1)S(1)}, f32[640,256]{1,0:T(8,128)S(1)}, f32[640,256]{1,0:T(8,128)S(1)}) custom-call(bf16[320,1024]{1,0:T(8,128)(2,1)S(1)} %copy-done.6, bf16[640,256]{1,0:T(8,128)(2,1)S(1)} %get-tuple-element.85.k_ref, bf16[640,256]{1,0:T(8,128)(2,1)S(1)} %get-tuple-element.84.v_ref, ...), custom_call_target="tpu_custom_call" | custom-call | flops 1677721600 | bytes 6553600 | tf_op jit(solution)/shard_map/attention_backward/pallas_call | solution.py:119
  155.8 5.9 %core_sum.2 = (bf16[512,1024]{1,0:T(8,128)(2,1)S(1)}, bf16[512,1024]{1,0:T(8,128)(2,1)}, bf16[512,1024]{1,0:T(8,128)(2,1)}, bf16[512,1024]{1,0:T(8,128)(2,1)S(1)}) custom-call(s32[8]{0:T(128)S(1)} %stack.44.index_ref, bf16[8,512,1024]{2,1,0:T(8,128)(2,1)} %bitcast.60, bf16[8,512,1024]{2,1,0:T(8,128)(2,1)} %bitcast.61, bf16[8,512,1024]{2,1,0:T(8,128)(2,1)} %bitcast.62, ...), custom_call_target="tpu_custom_call" | custom-call | flops 2097152 | bytes 12582912 | tf_op jit(solution)/shard_map/core_sum/pallas_call | solution.py:184
  162.7 1.8 collective-permute-done.1
  174.8 9.9 %reduce-scatter.3.cloned.1.call-done = bf16[80,4096]{1,0:T(8,128)(2,1)} async-done(((bf16[320,4096]{1,0:T(8,128)(2,1)}), bf16[80,4096]{1,0:T(8,128)(2,1)}) %reduce-scatter.3.cloned.1.call-update) | async-done | bytes 655376 | tf_op jit(solution)/shard_map/reduce_scatter | solution.py:144
  184.7 6.1 %collective-permute-done.3.refs_2_ = bf16[512,1024]{1,0:T(8,128)(2,1)} collective-permute-done((bf16[512,1024]{1,0:T(8,128)(2,1)}, bf16[512,1024]{1,0:T(8,128)(2,1)}, u32[]{:S(2)}, u32[]{:S(2)}) %collective-permute-start.3) | collective-permute-done | bytes 1048608 | tf_op jit(solution)/shard_map/ppermute | solution.py:206
  190.8 22.4 %collective-permute-done.4.refs_3_ = bf16[512,1024]{1,0:T(8,128)(2,1)} collective-permute-done((bf16[512,1024]{1,0:T(8,128)(2,1)}, bf16[512,1024]{1,0:T(8,128)(2,1)}, u32[]{:S(2)}, u32[]{:S(2)}) %collective-permute-start.4) | collective-permute-done | bytes 1048608 | tf_op jit(solution)/shard_map/ppermute | solution.py:206
  213.2 8.8 %convolution_convert_fusion = bf16[4096,1536]{1,0:T(8,128)(2,1)S(1)} fusion(bf16[320,1536]{1,0:T(8,128)(2,1)} %pad_maximum_fusion, bf16[320,4096]{1,0:T(8,128)(2,1)} %all-gather.3.cloned.1.call-done, f32[4096]{0:T(1024)S(1)} %copy-done.27, f32[320]{0:T(512)S(1)} %add_rsqrt_fusion), kind=kOutput, calls=%fused_computation | convolution fusion | flops 4038066176 | bytes 16205056 | tf_op jit(solution)/shard_map/dot_general | solution.py:37
  222.0 3.1 dynamic-slice_bitcast_fusion
  225.1 3.3 copy-done.12
  228.5 5.4 %fusion.26 = f32[320,4096]{1,0:T(8,128)S(1)} fusion(bf16[320,1024]{1,0:T(8,128)(2,1)S(1)} %copy-done.9, bf16[4096,1024]{1,0:T(8,128)(2,1)} %param.16), kind=kOutput, calls=%fused_computation.68 | convolution fusion | flops 2684354560 | bytes 14286848 | tf_op jit(solution)/shard_map/dot_general | solution.py:33
  235.4 2.4 fusion
  239.2 8.4 %core_sum.3 = (bf16[512,1536]{1,0:T(8,128)(2,1)S(1)}, bf16[512,1536]{1,0:T(8,128)(2,1)}, bf16[512,1536]{1,0:T(8,128)(2,1)}, bf16[512,1536]{1,0:T(8,128)(2,1)}) custom-call(s32[8]{0:T(128)S(1)} %stack.44.index_ref, bf16[8,512,1536]{2,1,0:T(8,128)(2,1)} %bitcast.55, bf16[8,512,1536]{2,1,0:T(8,128)(2,1)} %bitcast.56, bf16[8,512,1536]{2,1,0:T(8,128)(2,1)} %bitcast.57, ...), custom_call_target="tpu_custom_call" | custom-call | flops 3145728 | bytes 18874368 | tf_op jit(solution)/shard_map/core_sum/pallas_call | solution.py:184
  253.2 34.9 %reduce-scatter.5.cloned.1.call-done = bf16[80,4096]{1,0:T(8,128)(2,1)} async-done(((bf16[320,4096]{1,0:T(8,128)(2,1)}), bf16[80,4096]{1,0:T(8,128)(2,1)}) %reduce-scatter.5.cloned.1.call-update) | async-done | bytes 655376 | tf_op jit(solution)/shard_map/reduce_scatter | solution.py:144
  289.8 2.8 fusion.10
  292.6 6.6 %add_turned.1 = f32[1024,512]{1,0:T(8,128)} custom-call(bf16[512,1024]{1,0:T(8,128)(2,1)S(1)} %get-tuple-element.76.refs_0_, bf16[512,1024]{1,0:T(8,128)(2,1)} %collective-permute-done.5.refs_1_, bf16[512,1024]{1,0:T(8,128)(2,1)} %collective-permute-done.3.refs_2_, bf16[512,1024]{1,0:T(8,128)(2,1)} %collective-permute-done.4.refs_3_), custom_call_target="tpu_custom_call" | custom-call | tf_op jit(solution)/shard_map/add_turned/pallas_call | solution.py:219
  299.2 20.9 %collective-permute-done.8 = bf16[512,1536]{1,0:T(8,128)(2,1)} collective-permute-done((bf16[512,1536]{1,0:T(8,128)(2,1)}, bf16[512,1536]{1,0:T(8,128)(2,1)}, u32[]{:S(2)}, u32[]{:S(2)}) %collective-permute-start.8) | collective-permute-done | bytes 1572896 | tf_op jit(solution)/shard_map/ppermute | solution.py:206
  320.5 2.6 convert_add_fusion.1
  323.1 3.9 %convert_add_fusion = f32[512,1024]{1,0:T(8,128)} fusion(bf16[512,1536]{1,0:T(8,128)(2,1)} %collective-permute-done.9, bf16[512,1536]{1,0:T(8,128)(2,1)} %collective-permute-done.8, bf16[512,1536]{1,0:T(8,128)(2,1)} %collective-permute-done.7, bf16[512,1536]{1,0:T(8,128)(2,1)S(1)} %copy-done.4), kind=kLoop, calls=%fused_computation.13 | loop fusion | flops 3670016 | bytes 6291456 | tf_op jit(solution)/shard_map/add | solution.py:231
  (118 shorter events, 35.7 us)
Async XLA Ops:
  7.2 62.6 %copy-start = (bf16[4096,256]{1,0:T(8,128)(2,1)S(1)}, bf16[4096,256]{1,0:T(8,128)(2,1)}, u32[]{:S(2)}) copy-start(bf16[4096,256]{1,0:T(8,128)(2,1)} %param.17) | copy-start | bytes 6291460
  7.2 59.9 %all-gather.3.cloned.1.call-start = ((), (), s32[]{:S(2)}) async-start(), calls=%async_computation.2 | async-start | bytes 3276800 | tf_op jit(solution)/shard_map/all_gather | solution.py:140
  7.9 61.8 %copy-start.27 = (f32[4096]{0:T(1024)S(1)}, f32[4096]{0:T(1024)}, u32[]{:S(2)}) copy-start(f32[4096]{0:T(1024)} %param.15) | copy-start | bytes 49156
  7.9 114.4 %all-gather.5.cloned.1.call-start = ((), (), s32[]{:S(2)}) async-start(), calls=%async_computation.3 | async-start | bytes 3276800 | tf_op jit(solution)/shard_map/all_gather | solution.py:140
  67.2 117.6 %reduce-scatter.3.cloned.1.call-start = ((), (), s32[]{:S(2)}) async-start(), calls=%async_computation.4 | async-start | bytes 3276800 | tf_op jit(solution)/shard_map/reduce_scatter | solution.py:144
  67.2 2.5 copy-start.18
  75.3 22.1 %slice-start = ((s8[8388608]{0:T(1024)(128)(4,1)}), s8[4194304]{0:T(1024)(128)(4,1)S(1)}, s32[]{:S(2)}) async-start(s8[8388608]{0:T(1024)(128)(4,1)} %bitcast.68), calls=%async_computation.6 | async-start | bytes 8388608
  75.3 22.1 %slice-start.1 = ((s8[8388608]{0:T(1024)(128)(4,1)}), s8[4194304]{0:T(1024)(128)(4,1)S(1)}, s32[]{:S(2)}) async-start(s8[8388608]{0:T(1024)(128)(4,1)} %bitcast.68), calls=%async_computation.7 | async-start | bytes 8388608
  75.3 9.4 %collective-permute-start = (bf16[320,512]{1,0:T(8,128)(2,1)S(1)}, bf16[320,512]{1,0:T(8,128)(2,1)S(1)}, u32[]{:S(2)}, u32[]{:S(2)}) collective-permute-start(bf16[320,512]{1,0:T(8,128)(2,1)S(1)} %pad_maximum_fusion.2), channel_id=1, source_target_pairs={{0,4},{4,0},{1,5},{5,1},{2,6},{6,2},{3,7},{7,3},{8,12},{12,8},{9,1... | collective-permute-start | bytes 983048 | tf_op jit(solution)/shard_map/ppermute | solution.py:263
  92.9 2.8 copy-start.1
  128.8 4.8 %copy-start.13 = (bf16[4096,1024]{1,0:T(8,128)(2,1)}, bf16[4096,1024]{1,0:T(8,128)(2,1)S(1)}, u32[]{:S(2)}) copy-start(bf16[4096,1024]{1,0:T(8,128)(2,1)S(1)} %convolution_convert_fusion.1) | copy-start | bytes 25165828
  133.5 22.3 %collective-permute-start.2 = (bf16[2,1024,1024]{2,1,0:T(8,128)(2,1)}, bf16[2,1024,1024]{2,1,0:T(8,128)(2,1)}, u32[]{:S(2)}, u32[]{:S(2)}) collective-permute-start(bf16[2,1024,1024]{2,1,0:T(8,128)(2,1)} %dynamic-slice_bitcast_fusion.1), channel_id=1, source_target_pairs={{0,8},{8,0},{16,24},{24,16},{1,9},{9,1},{17,25},{25,17},{2,10},{10... | collective-permute-start | bytes 12582920 | tf_op jit(solution)/shard_map/ppermute | solution.py:156
  133.5 154.6 %reduce-scatter.5.cloned.1.call-start = ((), (), s32[]{:S(2)}) async-start(), calls=%async_computation.5 | async-start | bytes 3276800 | tf_op jit(solution)/shard_map/reduce_scatter | solution.py:144
  133.8 7.2 %copy-start.6 = (bf16[320,1024]{1,0:T(8,128)(2,1)S(1)}, bf16[320,1024]{1,0:T(8,128)(2,1)}, u32[]{:S(2)}) copy-start(bf16[320,1024]{1,0:T(8,128)(2,1)} %copy-done.5) | copy-start | bytes 1966084
  140.9 2.9 copy-start.2
  154.2 10.2 %collective-permute-start.1 = (bf16[320,512]{1,0:T(8,128)(2,1)S(1)}, bf16[320,512]{1,0:T(8,128)(2,1)}, u32[]{:S(2)}, u32[]{:S(2)}) collective-permute-start(bf16[320,512]{1,0:T(8,128)(2,1)S(1)} %slice.125), channel_id=1, source_target_pairs={{0,4},{4,0},{1,5},{5,1},{2,6},{6,2},{3,7},{7,3},{8,12},{12,8},{9,1... | collective-permute-start | bytes 983048 | tf_op jit(solution)/shard_map/ppermute | solution.py:283
  155.8 11.6 %copy-start.22 = (f32[640,512]{1,0:T(8,128)S(1)}, f32[640,512]{1,0:T(8,128)}, u32[]{:S(2)}) copy-start(f32[640,512]{1,0:T(8,128)} %copy-done.21) | copy-start | bytes 3932164
  164.5 26.4 %collective-permute-start.3 = (bf16[512,1024]{1,0:T(8,128)(2,1)}, bf16[512,1024]{1,0:T(8,128)(2,1)}, u32[]{:S(2)}, u32[]{:S(2)}) collective-permute-start(bf16[512,1024]{1,0:T(8,128)(2,1)} %get-tuple-element.57), channel_id=1, source_target_pairs={{0,16},{4,20},{8,24},{12,28},{16,0},{20,4},{24,8},{28,12},{1,17},{... | collective-permute-start | bytes 3145736 | tf_op jit(solution)/shard_map/ppermute | solution.py:206
  165.9 47.3 %collective-permute-start.4 = (bf16[512,1024]{1,0:T(8,128)(2,1)}, bf16[512,1024]{1,0:T(8,128)(2,1)}, u32[]{:S(2)}, u32[]{:S(2)}) collective-permute-start(bf16[512,1024]{1,0:T(8,128)(2,1)} %get-tuple-element.58), channel_id=1, source_target_pairs={{0,4},{4,0},{8,12},{12,8},{16,20},{20,16},{24,28},{28,24},{1,5},{5... | collective-permute-start | bytes 3145736 | tf_op jit(solution)/shard_map/ppermute | solution.py:206
  171.3 2.4 copy-start.15
  171.3 2.5 copy-start.8
  171.3 2.5 copy-start.23
  171.3 57.1 %collective-permute-start.5 = (bf16[512,1024]{1,0:T(8,128)(2,1)}, bf16[512,1024]{1,0:T(8,128)(2,1)}, u32[]{:S(2)}, u32[]{:S(2)}) collective-permute-start(bf16[512,1024]{1,0:T(8,128)(2,1)} %copy-done.10), channel_id=1, source_target_pairs={{0,20},{4,16},{8,28},{12,24},{16,4},{20,0},{24,12},{28,8},{1,21},{... | collective-permute-start | bytes 3145736 | tf_op jit(solution)/shard_map/ppermute | solution.py:206
  222.0 6.4 %copy-start.12 = (bf16[4096,1536]{1,0:T(8,128)(2,1)}, bf16[4096,1536]{1,0:T(8,128)(2,1)S(1)}, u32[]{:S(2)}) copy-start(bf16[4096,1536]{1,0:T(8,128)(2,1)S(1)} %convolution_convert_fusion) | copy-start | bytes 37748740
  222.0 6.4 %copy-start.9 = (bf16[320,1024]{1,0:T(8,128)(2,1)S(1)}, bf16[320,1024]{1,0:T(8,128)(2,1)}, u32[]{:S(2)}) copy-start(bf16[320,1024]{1,0:T(8,128)(2,1)} %copy-done.7) | copy-start | bytes 1966084
  228.5 10.7 %collective-permute-start.6 = (bf16[2,1024,1536]{2,1,0:T(8,128)(2,1)}, bf16[2,1024,1536]{2,1,0:T(8,128)(2,1)}, u32[]{:S(2)}, u32[]{:S(2)}) collective-permute-start(bf16[2,1024,1536]{2,1,0:T(8,128)(2,1)} %dynamic-slice_bitcast_fusion), channel_id=1, source_target_pairs={{0,8},{8,0},{16,24},{24,16},{1,9},{9,1},{17,25},{25,17},{2,10},{10... | collective-permute-start | bytes 18874376 | tf_op jit(solution)/shard_map/ppermute | solution.py:156
  239.2 13.1 %copy-start.25 = (bf16[80,4096]{1,0:T(8,128)(2,1)S(1)}, bf16[80,4096]{1,0:T(8,128)(2,1)}, u32[]{:S(2)}) copy-start(bf16[80,4096]{1,0:T(8,128)(2,1)} %param.11) | copy-start | bytes 1966084
  239.2 13.1 %copy-start.26 = (bf16[80,4096]{1,0:T(8,128)(2,1)S(1)}, bf16[80,4096]{1,0:T(8,128)(2,1)}, u32[]{:S(2)}) copy-start(bf16[80,4096]{1,0:T(8,128)(2,1)} %reduce-scatter.3.cloned.1.call-done) | copy-start | bytes 1966084
  248.7 50.5 %collective-permute-start.7 = (bf16[512,1536]{1,0:T(8,128)(2,1)}, bf16[512,1536]{1,0:T(8,128)(2,1)}, u32[]{:S(2)}, u32[]{:S(2)}) collective-permute-start(bf16[512,1536]{1,0:T(8,128)(2,1)} %get-tuple-element.73), channel_id=1, source_target_pairs={{0,20},{4,16},{8,28},{12,24},{16,4},{20,0},{24,12},{28,8},{1,21},{... | collective-permute-start | bytes 4718600 | tf_op jit(solution)/shard_map/ppermute | solution.py:206
  249.6 70.6 %collective-permute-start.8 = (bf16[512,1536]{1,0:T(8,128)(2,1)}, bf16[512,1536]{1,0:T(8,128)(2,1)}, u32[]{:S(2)}, u32[]{:S(2)}) collective-permute-start(bf16[512,1536]{1,0:T(8,128)(2,1)} %get-tuple-element.74), channel_id=1, source_target_pairs={{0,16},{4,20},{8,24},{12,28},{16,0},{20,4},{24,8},{28,12},{1,17},{... | collective-permute-start | bytes 4718600 | tf_op jit(solution)/shard_map/ppermute | solution.py:206
  251.0 69.5 %collective-permute-start.9 = (bf16[512,1536]{1,0:T(8,128)(2,1)}, bf16[512,1536]{1,0:T(8,128)(2,1)}, u32[]{:S(2)}, u32[]{:S(2)}) collective-permute-start(bf16[512,1536]{1,0:T(8,128)(2,1)} %get-tuple-element.75), channel_id=1, source_target_pairs={{0,4},{4,0},{8,12},{12,8},{16,20},{20,16},{24,28},{28,24},{1,5},{5... | collective-permute-start | bytes 4718600 | tf_op jit(solution)/shard_map/ppermute | solution.py:206
  292.6 27.9 %copy-start.4 = (bf16[512,1536]{1,0:T(8,128)(2,1)S(1)}, bf16[512,1536]{1,0:T(8,128)(2,1)}, u32[]{:S(2)}) copy-start(bf16[512,1536]{1,0:T(8,128)(2,1)} %copy-done.3) | copy-start | bytes 4718596
  (12 other events, 14.7 us)
Sparse Core Ops, SparseCore 0:
  9.6 57.4 all-gather.2
  68.7 53.5 all-gather.4
  133.7 51.0 reduce-scatter.2
  237.9 50.1 reduce-scatter.4
